TPU v7x, 256 devices: a whole 4x4x8 slice. The times are simulated.
256 devices in a mesh: wide: 64 (over x, z, y_lo), narrow: 4 (over y_hi, core).
Axes of the slice: x: 4, y: 4 (y_hi: 2, y_lo: 2; y = y_hi * 2 + y_lo), z: 8, core: 2. Of those that a mesh axis runs over, the one named last changes fastest.
Arguments:
- queries: bfloat16 [32768, 8192], P(('wide', 'narrow')), may hold values from -10 to 10
- keys: bfloat16 [32768, 512], P(('wide', 'narrow')), may hold values from -10 to 10
- values: bfloat16 [32768, 512], P(('wide', 'narrow')), may hold values from -6 to 6
- block_order: int32 [64, 2], replicated, may hold values from 0 to 127, as said below
- doc_lengths: int32 [64], replicated, may hold values from 1 to 768, 32768 in all
Outputs:
- attended: float32 [32768, 8192], P(('wide', 'narrow'))
Inputs may be any that keep to these rules, and one draw needn't show every extreme that they name: `block_order`: row w holds the two blocks w and 2 * 64 - 1 - w, in either order.
All inputs are finite; a program needn't handle non-finite values.
Results may differ from a plain program's by a relative error of at most 0.002.
Values may be sent and summed in bfloat16 or wider, within the bound.
A program may use at most 128 MiB of HBM per device.

v0:
```python
import math

import jax
import jax.numpy as jnp
from jax import lax
from jax.sharding import PartitionSpec as P

QUERY_HEADS = 64
KV_HEADS = 4
HEAD_DIM = 128
REACH = 3


def from_behind(block, axis, distance):
    devices = range(lax.axis_size(axis))
    route = [(i - distance, i) for i in devices if i - distance in devices]
    return lax.ppermute(block, axis, route)


def doc_index(positions, doc_ends):
    return jnp.sum((positions[:, None] >= doc_ends[None, :]).astype(jnp.int32), axis=1)


def locate(block_table, target, own_index):
    wide_ids = jnp.arange(block_table.shape[0], dtype=jnp.int32)[:, None]
    slot_ids = jnp.arange(2, dtype=jnp.int32)[None, :]
    matches = block_table == target
    device_id = jnp.sum(jnp.where(matches, wide_ids, 0))
    slot_id = jnp.sum(jnp.where(matches, slot_ids, 0))
    return (jnp.clip(device_id - own_index + REACH, 0, 2 * REACH), slot_id)


def attend(q_tile, q_pos, block_id, candidates, block_table, doc_ends, own_index, group_rows):
    half_rows = q_tile.shape[0]
    score_scale = 1.0 / math.sqrt(HEAD_DIM)
    q_doc = doc_index(q_pos, doc_ends)
    score_tiles = []
    value_tiles = []
    seen_flags = []
    for distance in range(REACH + 1):
        target = block_id - distance
        offset_id, slot_id = locate(block_table, target, own_index)
        k_tile = candidates[offset_id, 0, slot_id].reshape(group_rows, KV_HEADS, HEAD_DIM)
        v_tile = candidates[offset_id, 1, slot_id].reshape(group_rows, KV_HEADS, HEAD_DIM)
        k_pos = target * group_rows + jnp.arange(group_rows, dtype=jnp.int32)
        visible = (
            (k_pos[None, :] <= q_pos[:, None])
            & (doc_index(k_pos, doc_ends)[None, :] == q_doc[:, None])
            & (target >= 0)
        )

        def score_tile(k_tile=k_tile, visible=visible):
            raw_scores = (
                jnp.einsum("qhgd,khd->hgqk", q_tile, k_tile, preferred_element_type=jnp.float32)
                * score_scale
            )
            return jnp.where(visible[None, None], raw_scores, -1e30)

        any_seen = jnp.any(visible)
        score_tiles.append(score_tile())
        value_tiles.append(v_tile)
        seen_flags.append(any_seen)
    scores = jnp.concatenate(score_tiles, axis=-1)
    row_max = jnp.max(scores, axis=-1, keepdims=True)
    weights = jnp.exp(scores - row_max)
    weight_sum = jnp.sum(weights, axis=-1, keepdims=True)
    rounded = weights.astype(jnp.bfloat16)
    all_values = jnp.concatenate(value_tiles, axis=0)
    mixed_out = jnp.einsum(
        "hgqk,khd->hgqd", rounded, all_values, preferred_element_type=jnp.float32
    )
    mixed_out = mixed_out / weight_sum
    return mixed_out.transpose(2, 0, 1, 3).reshape(half_rows, QUERY_HEADS * HEAD_DIM)


def body(queries, keys, values, block_order, doc_lengths):
    row_count = queries.shape[0]
    half_rows = row_count // 2
    narrow_count = lax.axis_size("narrow")
    group_rows = narrow_count * half_rows
    kv_width = keys.shape[1]
    head_share = QUERY_HEADS // KV_HEADS
    own_index = lax.axis_index("wide")
    member_index = lax.axis_index("narrow")
    kv_local = jnp.stack([keys, values])
    kv_whole = lax.all_gather(kv_local, "narrow", axis=1, tiled=True)
    kv_panel = kv_whole.reshape(2, narrow_count, 2, half_rows, kv_width).transpose(0, 2, 1, 3, 4)
    kv_panel = kv_panel.reshape(2, 2, group_rows, kv_width)
    early_slot = (block_order[own_index, 0] >= block_order.shape[0]).astype(jnp.int32)
    early_half = lax.dynamic_index_in_dim(kv_panel, early_slot, 1, keepdims=False)
    from_lower = early_half
    from_upper = kv_panel
    lower_list = []
    upper_list = []
    for hop_index in range(REACH):
        from_lower = from_behind(from_lower, "wide", 1)
        from_upper = from_behind(from_upper, "wide", -1)
        lower_list.append(jnp.stack([from_lower, from_lower], axis=1))
        upper_list.append(from_upper)
    candidates = jnp.stack(lower_list[::-1] + [kv_panel] + upper_list)
    doc_ends = jnp.cumsum(doc_lengths)
    outputs = []
    for slot_index in range(2):
        block_id = block_order[own_index, slot_index]
        q_pos = (
            block_id * group_rows
            + member_index * half_rows
            + jnp.arange(half_rows, dtype=jnp.int32)
        )
        q_tile = queries[slot_index * half_rows : (slot_index + 1) * half_rows]
        q_tile = q_tile.reshape(half_rows, KV_HEADS, head_share, HEAD_DIM)
        outputs.append(
            attend(
                q_tile, q_pos, block_id, candidates, block_order, doc_ends, own_index, group_rows
            )
        )
    return jnp.concatenate(outputs, axis=0)


def solution(mesh):
    in_specs = (
        P(("wide", "narrow"), None),
        P(("wide", "narrow"), None),
        P(("wide", "narrow"), None),
        P(),
        P(),
    )
    out_specs = P(("wide", "narrow"), None)
    return jax.shard_map(body, mesh=mesh, in_specs=in_specs, out_specs=out_specs, check_vma=False)
```

profile of v0, /device:TPU:6, one launch (start us, length us, event | category | flops | bytes accessed | tf_op | source)
XLA Modules:
  0.0 242.6 jit_solution(14232062501103277647)
XLA Ops:
  8.3 27.2 %all-gather.2.cloned.1.call-done = bf16[2,512,512]{2,1,0:T(8,128)(2,1)} async-done(((bf16[2,128,512]{2,1,0:T(8,128)(2,1)}), bf16[2,512,512]{2,1,0:T(8,128)(2,1)}) %all-gather.2.cloned.1.call-update) | async-done | bytes 1048592 | tf_op jit(solution)/shard_map/all_gather | solution.py:86
  36.8 5.5 %collective-permute-start.3 = (bf16[2,2,256,512]{3,2,1,0:T(8,128)(2,1)S(1)}, bf16[2,2,256,512]{3,2,1,0:T(8,128)(2,1)}, u32[]{:S(2)}, u32[]{:S(2)}) collective-permute-start(bf16[2,2,256,512]{3,2,1,0:T(8,128)(2,1)S(1)} %bitcast.149), channel_id=1, source_target_pairs={{4,0},{8,4},{12,8},{16,12},{20,16},{24,20},{28,24},{32,28},{36,32}... | collective-permute-start | bytes 3145736 | tf_op jit(solution)/shard_map/ppermute | solution.py:17
  49.0 1.9 collective-permute-start
  51.0 2.8 %select_reduce_fusion.12 = (s32[]{:T(128)}, s32[]{:T(128)}, s32[]{:T(128)}, s32[]{:T(128)}, s32[]{:T(128)}, /*index=5*/s32[]{:T(128)}, s32[]{:T(128)}, s32[]{:T(...) fusion(s32[64,2]{0,1:T(2,128)} %param.8, ...), kind=kLoop, calls=%fused_computation.115 | loop fusion | flops 5104 | bytes 608 | tf_op jit(solution)/shard_map/reduce_sum | solution.py:29
  53.8 2.7 %slice_bitcast_fusion.1 = (bf16[8,8,64,128]{3,1,2,0:T(8,128)(2,1)S(1)}, bf16[8,8,64,128]{3,1,2,0:T(8,128)(2,1)}) fusion(bf16[128,8192]{1,0:T(8,128)(2,1)} %param.5), kind=kLoop, calls=%fused_computation.47 | loop fusion | bytes 4194304
  56.5 17.7 %collective-permute-done = bf16[2,256,512]{2,1,0:T(8,128)(2,1)} collective-permute-done((bf16[2,256,512]{2,1,0:T(8,128)(2,1)S(1)}, bf16[2,256,512]{2,1,0:T(8,128)(2,1)}, u32[]{:S(2)}, u32[]{:S(2)}) %collective-permute-start) | collective-permute-done | bytes 524320 | tf_op jit(solution)/shard_map/ppermute | solution.py:17
  74.2 4.5 %collective-permute-start.1 = (bf16[2,256,512]{2,1,0:T(8,128)(2,1)}, bf16[2,256,512]{2,1,0:T(8,128)(2,1)}, u32[]{:S(2)}, u32[]{:S(2)}) collective-permute-start(bf16[2,256,512]{2,1,0:T(8,128)(2,1)} %collective-permute-done), channel_id=1, source_target_pairs={{0,4},{4,8},{8,12},{12,16},{16,20},{20,24},{24,28},{28,32},{32,36}... | collective-permute-start | bytes 1572872 | tf_op jit(solution)/shard_map/ppermute | solution.py:17
  78.7 7.1 %collective-permute-start.4 = (bf16[2,2,256,512]{3,2,1,0:T(8,128)(2,1)}, bf16[2,2,256,512]{3,2,1,0:T(8,128)(2,1)}, u32[]{:S(2)}, u32[]{:S(2)}) collective-permute-start(bf16[2,2,256,512]{3,2,1,0:T(8,128)(2,1)} %collective-permute-done.3), channel_id=1, source_target_pairs={{4,0},{8,4},{12,8},{16,12},{20,16},{24,20},{28,24},{32,28},{36,32}... | collective-permute-start | bytes 3145736 | tf_op jit(solution)/shard_map/ppermute | solution.py:17
  109.0 3.9 %collective-permute-done.1 = bf16[2,256,512]{2,1,0:T(8,128)(2,1)} collective-permute-done((bf16[2,256,512]{2,1,0:T(8,128)(2,1)}, bf16[2,256,512]{2,1,0:T(8,128)(2,1)}, u32[]{:S(2)}, u32[]{:S(2)}) %collective-permute-start.1) | collective-permute-done | bytes 524320 | tf_op jit(solution)/shard_map/ppermute | solution.py:17
  112.9 4.4 %collective-permute-start.2 = (bf16[2,256,512]{2,1,0:T(8,128)(2,1)}, bf16[2,256,512]{2,1,0:T(8,128)(2,1)S(1)}, u32[]{:S(2)}, u32[]{:S(2)}) collective-permute-start(bf16[2,256,512]{2,1,0:T(8,128)(2,1)} %collective-permute-done.1), channel_id=1, source_target_pairs={{0,4},{4,8},{8,12},{12,16},{16,20},{20,24},{24,28},{28,32},{32,36}... | collective-permute-start | bytes 1572872 | tf_op jit(solution)/shard_map/ppermute | solution.py:17
  117.7 7.0 %collective-permute-start.5 = (bf16[2,2,256,512]{3,2,1,0:T(8,128)(2,1)}, bf16[2,2,256,512]{3,2,1,0:T(8,128)(2,1)S(1)}, u32[]{:S(2)}, u32[]{:S(2)}) collective-permute-start(bf16[2,2,256,512]{3,2,1,0:T(8,128)(2,1)} %collective-permute-done.4), channel_id=1, source_target_pairs={{4,0},{8,4},{12,8},{16,12},{20,16},{24,20},{28,24},{32,28},{36,32}... | collective-permute-start | bytes 3145736 | tf_op jit(solution)/shard_map/ppermute | solution.py:17
  124.8 25.8 %collective-permute-done.2 = bf16[2,256,512]{2,1,0:T(8,128)(2,1)S(1)} collective-permute-done((bf16[2,256,512]{2,1,0:T(8,128)(2,1)}, bf16[2,256,512]{2,1,0:T(8,128)(2,1)S(1)}, u32[]{:S(2)}, u32[]{:S(2)}) %collective-permute-start.2) | collective-permute-done | bytes 524320 | tf_op jit(solution)/shard_map/ppermute | solution.py:17
  157.6 1.8 copy.115
  159.4 1.8 copy.112
  163.0 1.8 copy.109
  165.6 1.8 copy.122
  170.4 2.3 fusion.43
  176.9 3.4 %fusion.8 = f32[4,16,64]{2,1,0:T(8,128)S(1)} fusion(f32[4,16,64]{2,1,0:T(8,128)S(1)} %maximum_maximum_fusion.1, f32[4,16,64,256]{3,2,1,0:T(8,128)S(1)} %get-tuple-element.68, f32[4,16,64,256]{3,2,1,0:T(8,128)S(1)} %get-tuple-element.70, f32[4,16,64,256]{3,2,1,0:T(8,128)S(1)} %get-tuple-element.74, f32[4,16,64,256]{3,2,1,0:T(8,128)S(1)} %get-tuple-element.72), kind=kLoop, calls=%fused_computation.9 | loop fusion | flops 20967424 | bytes 16809984 | tf_op jit(solution)/shard_map/reduce_sum | solution.py:66
  180.3 7.8 %bitcast_divide_fusion.1 = f32[64,4,16,128]{3,0,2,1:T(8,128)S(1)} fusion(f32[4,16,64]{2,1,0:T(8,128)S(1)} %maximum_maximum_fusion.1, f32[4,16,64,256]{3,2,1,0:T(8,128)} %copy-done, f32[4,16,64,256]{3,2,1,0:T(8,128)} %copy-done.2, f32[4,16,64,256]{3,2,1,0:T(8,128)} %copy-done.6, f32[4,16,64,256]{3,2,1,0:T(8,128)} %copy-done.4, ...), kind=kOutput, calls=%fused_computation.22 | convolution fusion | flops 1099431936 | bytes 19955712 | tf_op jit(solution)/shard_map/hgqk,khd->hgqd/dot_general | solution.py:69
  194.0 1.8 copy.130
  195.8 1.8 copy.136
  197.6 1.8 copy.139
  199.4 1.8 copy.143
  203.0 1.8 copy.144
  204.8 1.8 copy.141
  206.6 1.8 copy.145
  209.2 1.8 copy.146
  211.1 2.3 fusion.40
  217.6 3.2 %fusion.6 = f32[4,16,64]{2,1,0:T(8,128)S(1)} fusion(f32[4,16,64]{2,1,0:T(8,128)S(1)} %maximum_maximum_fusion, f32[4,16,64,256]{3,2,1,0:T(8,128)S(1)} %get-tuple-element.60, f32[4,16,64,256]{3,2,1,0:T(8,128)S(1)} %get-tuple-element.62, f32[4,16,64,256]{3,2,1,0:T(8,128)S(1)} %get-tuple-element.66, f32[4,16,64,256]{3,2,1,0:T(8,128)S(1)} %get-tuple-element.64), kind=kLoop, calls=%fused_computation.8 | loop fusion | flops 20967424 | bytes 16809984 | tf_op jit(solution)/shard_map/reduce_sum | solution.py:66
  220.8 8.5 %bitcast_divide_fusion = f32[64,4,16,128]{3,0,2,1:T(8,128)} fusion(f32[4,16,64]{2,1,0:T(8,128)S(1)} %maximum_maximum_fusion, f32[4,16,64,256]{3,2,1,0:T(8,128)} %copy-done.7, f32[4,16,64,256]{3,2,1,0:T(8,128)} %copy-done.1, f32[4,16,64,256]{3,2,1,0:T(8,128)} %copy-done.5, f32[4,16,64,256]{3,2,1,0:T(8,128)} %copy-done.3, ...), kind=kOutput, calls=%fused_computation.21 | convolution fusion | flops 1099431936 | bytes 19955712 | tf_op jit(solution)/shard_map/hgqk,khd->hgqd/dot_general | solution.py:69
  229.3 2.8 %copy.147 = f32[64,4,16,128]{3,2,1,0:T(8,128)S(1)} copy(f32[64,4,16,128]{3,0,2,1:T(8,128)} %bitcast_divide_fusion) | data formatting | bytes 4194304 | tf_op jit(solution)/shard_map/div | solution.py:72
  233.4 2.4 pad_maximum_fusion
  (92 shorter events, 37.6 us)
Async XLA Ops:
  6.5 95.2 %copy-start.18 = (s32[64]{0:T(128)S(1)}, s32[64]{0:T(128)}, u32[]{:S(2)}) copy-start(s32[64]{0:T(128)} %param.9) | copy-start | bytes 772
  6.5 28.9 %all-gather.2.cloned.1.call-start = ((), (), s32[]{:S(2)}) async-start(), calls=%async_computation | async-start | bytes 1310720 | tf_op jit(solution)/shard_map/all_gather | solution.py:86
  36.8 41.9 %collective-permute-start.3 = (bf16[2,2,256,512]{3,2,1,0:T(8,128)(2,1)S(1)}, bf16[2,2,256,512]{3,2,1,0:T(8,128)(2,1)}, u32[]{:S(2)}, u32[]{:S(2)}) collective-permute-start(bf16[2,2,256,512]{3,2,1,0:T(8,128)(2,1)S(1)} %bitcast.149), channel_id=1, source_target_pairs={{4,0},{8,4},{12,8},{16,12},{20,16},{24,20},{28,24},{32,28},{36,32}... | collective-permute-start | bytes 3145736 | tf_op jit(solution)/shard_map/ppermute | solution.py:17
  49.0 25.2 %collective-permute-start = (bf16[2,256,512]{2,1,0:T(8,128)(2,1)S(1)}, bf16[2,256,512]{2,1,0:T(8,128)(2,1)}, u32[]{:S(2)}, u32[]{:S(2)}) collective-permute-start(bf16[2,256,512]{2,1,0:T(8,128)(2,1)S(1)} %dynamic-slice_bitcast_fusion), channel_id=1, source_target_pairs={{0,4},{4,8},{8,12},{12,16},{16,20},{20,24},{24,28},{28,32},{32,36}... | collective-permute-start | bytes 1572872 | tf_op jit(solution)/shard_map/ppermute | solution.py:17
  74.2 38.6 %collective-permute-start.1 = (bf16[2,256,512]{2,1,0:T(8,128)(2,1)}, bf16[2,256,512]{2,1,0:T(8,128)(2,1)}, u32[]{:S(2)}, u32[]{:S(2)}) collective-permute-start(bf16[2,256,512]{2,1,0:T(8,128)(2,1)} %collective-permute-done), channel_id=1, source_target_pairs={{0,4},{4,8},{8,12},{12,16},{16,20},{20,24},{24,28},{28,32},{32,36}... | collective-permute-start | bytes 1572872 | tf_op jit(solution)/shard_map/ppermute | solution.py:17
  78.7 39.0 %collective-permute-start.4 = (bf16[2,2,256,512]{3,2,1,0:T(8,128)(2,1)}, bf16[2,2,256,512]{3,2,1,0:T(8,128)(2,1)}, u32[]{:S(2)}, u32[]{:S(2)}) collective-permute-start(bf16[2,2,256,512]{3,2,1,0:T(8,128)(2,1)} %collective-permute-done.3), channel_id=1, source_target_pairs={{4,0},{8,4},{12,8},{16,12},{20,16},{24,20},{28,24},{32,28},{36,32}... | collective-permute-start | bytes 3145736 | tf_op jit(solution)/shard_map/ppermute | solution.py:17
  112.9 37.7 %collective-permute-start.2 = (bf16[2,256,512]{2,1,0:T(8,128)(2,1)}, bf16[2,256,512]{2,1,0:T(8,128)(2,1)S(1)}, u32[]{:S(2)}, u32[]{:S(2)}) collective-permute-start(bf16[2,256,512]{2,1,0:T(8,128)(2,1)} %collective-permute-done.1), channel_id=1, source_target_pairs={{0,4},{4,8},{8,12},{12,16},{16,20},{20,24},{24,28},{28,32},{32,36}... | collective-permute-start | bytes 1572872 | tf_op jit(solution)/shard_map/ppermute | solution.py:17
  117.7 38.2 %collective-permute-start.5 = (bf16[2,2,256,512]{3,2,1,0:T(8,128)(2,1)}, bf16[2,2,256,512]{3,2,1,0:T(8,128)(2,1)S(1)}, u32[]{:S(2)}, u32[]{:S(2)}) collective-permute-start(bf16[2,2,256,512]{3,2,1,0:T(8,128)(2,1)} %collective-permute-done.4), channel_id=1, source_target_pairs={{4,0},{8,4},{12,8},{16,12},{20,16},{24,20},{28,24},{32,28},{36,32}... | collective-permute-start | bytes 3145736 | tf_op jit(solution)/shard_map/ppermute | solution.py:17
  168.4 4.3 %copy-start.13 = (bf16[1,1,1,256,512]{3,4,2,1,0:T(8,128)(2,1)S(1)}, bf16[1,1,1,256,512]{3,4,2,1,0:T(8,128)(2,1)}, u32[]{:S(2)}) copy-start(bf16[1,1,1,256,512]{3,4,2,1,0:T(8,128)(2,1)} %copy.112) | copy-start | bytes 786436
  170.4 3.7 %copy-start.11 = (bf16[1,1,1,256,512]{3,4,2,1,0:T(8,128)(2,1)S(1)}, bf16[1,1,1,256,512]{3,4,2,1,0:T(8,128)(2,1)}, u32[]{:S(2)}) copy-start(bf16[1,1,1,256,512]{3,4,2,1,0:T(8,128)(2,1)} %copy.106) | copy-start | bytes 786436
  172.7 4.1 %copy-start = (f32[4,16,64,256]{3,2,1,0:T(8,128)}, f32[4,16,64,256]{3,2,1,0:T(8,128)S(1)}, u32[]{:S(2)}) copy-start(f32[4,16,64,256]{3,2,1,0:T(8,128)S(1)} %get-tuple-element.68) | copy-start | bytes 12582916
  172.8 2.7 %copy-start.9 = (bf16[1,1,1,256,512]{3,4,2,1,0:T(8,128)(2,1)S(1)}, bf16[1,1,1,256,512]{3,4,2,1,0:T(8,128)(2,1)}, u32[]{:S(2)}) copy-start(bf16[1,1,1,256,512]{3,4,2,1,0:T(8,128)(2,1)} %copy.109) | copy-start | bytes 786436
  174.1 2.8 %copy-start.2 = (f32[4,16,64,256]{3,2,1,0:T(8,128)}, f32[4,16,64,256]{3,2,1,0:T(8,128)S(1)}, u32[]{:S(2)}) copy-start(f32[4,16,64,256]{3,2,1,0:T(8,128)S(1)} %get-tuple-element.70) | copy-start | bytes 12582916
  175.5 4.8 %copy-start.4 = (f32[4,16,64,256]{3,2,1,0:T(8,128)}, f32[4,16,64,256]{3,2,1,0:T(8,128)S(1)}, u32[]{:S(2)}) copy-start(f32[4,16,64,256]{3,2,1,0:T(8,128)S(1)} %get-tuple-element.72) | copy-start | bytes 12582916
  176.8 3.4 %copy-start.6 = (f32[4,16,64,256]{3,2,1,0:T(8,128)}, f32[4,16,64,256]{3,2,1,0:T(8,128)S(1)}, u32[]{:S(2)}) copy-start(f32[4,16,64,256]{3,2,1,0:T(8,128)S(1)} %get-tuple-element.74) | copy-start | bytes 12582916
  209.2 4.2 %copy-start.12 = (bf16[1,1,1,256,512]{3,4,2,1,0:T(8,128)(2,1)S(1)}, bf16[1,1,1,256,512]{3,4,2,1,0:T(8,128)(2,1)}, u32[]{:S(2)}) copy-start(bf16[1,1,1,256,512]{3,4,2,1,0:T(8,128)(2,1)} %copy.127) | copy-start | bytes 786436
  211.1 3.7 %copy-start.10 = (bf16[1,1,1,256,512]{3,4,2,1,0:T(8,128)(2,1)S(1)}, bf16[1,1,1,256,512]{3,4,2,1,0:T(8,128)(2,1)}, u32[]{:S(2)}) copy-start(bf16[1,1,1,256,512]{3,4,2,1,0:T(8,128)(2,1)} %copy.130) | copy-start | bytes 786436
  213.4 4.1 %copy-start.1 = (f32[4,16,64,256]{3,2,1,0:T(8,128)}, f32[4,16,64,256]{3,2,1,0:T(8,128)S(1)}, u32[]{:S(2)}) copy-start(f32[4,16,64,256]{3,2,1,0:T(8,128)S(1)} %get-tuple-element.62) | copy-start | bytes 12582916
  213.4 2.7 %copy-start.8 = (bf16[1,1,1,256,512]{3,4,2,1,0:T(8,128)(2,1)S(1)}, bf16[1,1,1,256,512]{3,4,2,1,0:T(8,128)(2,1)}, u32[]{:S(2)}) copy-start(bf16[1,1,1,256,512]{3,4,2,1,0:T(8,128)(2,1)} %copy.136) | copy-start | bytes 786436
  214.8 2.8 %copy-start.3 = (f32[4,16,64,256]{3,2,1,0:T(8,128)}, f32[4,16,64,256]{3,2,1,0:T(8,128)S(1)}, u32[]{:S(2)}) copy-start(f32[4,16,64,256]{3,2,1,0:T(8,128)S(1)} %get-tuple-element.64) | copy-start | bytes 12582916
  216.1 4.7 %copy-start.5 = (f32[4,16,64,256]{3,2,1,0:T(8,128)}, f32[4,16,64,256]{3,2,1,0:T(8,128)S(1)}, u32[]{:S(2)}) copy-start(f32[4,16,64,256]{3,2,1,0:T(8,128)S(1)} %get-tuple-element.66) | copy-start | bytes 12582916
  217.5 3.3 %copy-start.7 = (f32[4,16,64,256]{3,2,1,0:T(8,128)}, f32[4,16,64,256]{3,2,1,0:T(8,128)S(1)}, u32[]{:S(2)}) copy-start(f32[4,16,64,256]{3,2,1,0:T(8,128)S(1)} %get-tuple-element.60) | copy-start | bytes 12582916
  217.6 3.3 %copy-start.14 = (bf16[256,4,128]{2,0,1:T(8,128)(2,1)S(1)}, bf16[256,4,128]{2,0,1:T(8,128)(2,1)}, u32[]{:S(2)}) copy-start(bf16[256,4,128]{2,0,1:T(8,128)(2,1)} %copy.143) | copy-start | bytes 786436
  217.6 3.3 %copy-start.15 = (bf16[256,4,128]{2,0,1:T(8,128)(2,1)S(1)}, bf16[256,4,128]{2,0,1:T(8,128)(2,1)}, u32[]{:S(2)}) copy-start(bf16[256,4,128]{2,0,1:T(8,128)(2,1)} %copy.144) | copy-start | bytes 786436
  217.6 3.3 %copy-start.16 = (bf16[256,4,128]{2,0,1:T(8,128)(2,1)S(1)}, bf16[256,4,128]{2,0,1:T(8,128)(2,1)}, u32[]{:S(2)}) copy-start(bf16[256,4,128]{2,0,1:T(8,128)(2,1)} %copy.145) | copy-start | bytes 786436
  217.6 3.3 %copy-start.17 = (bf16[256,4,128]{2,0,1:T(8,128)(2,1)S(1)}, bf16[256,4,128]{2,0,1:T(8,128)(2,1)}, u32[]{:S(2)}) copy-start(bf16[256,4,128]{2,0,1:T(8,128)(2,1)} %copy.146) | copy-start | bytes 786436
Sparse Core Ops, SparseCore 0:
  9.2 26.2 all-gather.1
where the time goes:
time: 245 us; the launch traced here: 243 us
  waiting for transfers between devices  74.6 us (30%)
  local copies, waits for them, and re-layouts  51.5 us (21%)
  between operations  40.2 us (16%)
  starting transfers between devices  30.4 us (12%)
  matrix products  29 us (12%)
  other arithmetic  17 us (7%)
    ppermute x6, waiting for transfers between devices, from_behind(): return lax.ppermute(block, axis, route)  47.4 us
    ppermute x6, starting transfers between devices, from_behind(): return lax.ppermute(block, axis, route)  30.4 us
    all_gather x1, waiting for transfers between devices, body(): kv_whole = lax.all_gather(kv_local, 'narrow', axis=1, tiled=True)  27.2 us
    dot_general x2, matrix products, attend(): jnp.einsum('hgqk,khd->hgqd', rounded, all_values, preferred_element_type=...  16.3 us
    dynamic_slice x8, local copies, waits for them, and re-layouts, attend(): candidates[offset_id, 0, slot_id].reshape(group_rows, KV_HEADS, HEAD_DIM)  14.3 us
    dot_general x8, matrix products, score_tile(): jnp.einsum('qhgd,khd->hgqk', q_tile, k_tile, preferred_element_type=jnp.f...  12.7 us
    another operation x8, local copies, waits for them, and re-layouts, attend(): candidates[offset_id, 1, slot_id].reshape(group_rows, KV_HEADS, HEAD_DIM)  11.6 us
    unnamed x46, local copies, waits for them, and re-layouts  9.6 us
  transfers between devices with their start and end apart: 7, of which 4 were waited for; matrix products, arithmetic and copies ran while one was open for 6% of the time, Pallas kernels for 0%

commit v1 on v0

v1 whole, which is shorter than its diff:
```python
import functools
import math

import jax
import jax.numpy as jnp
from jax import lax
from jax.experimental import pallas as pl
from jax.experimental.pallas import tpu as pltpu
from jax.sharding import PartitionSpec as P

MESH = pl.DeviceIdType.MESH
QUERY_HEADS = 64
KV_HEADS = 4
HEAD_DIM = 128
SHARE = QUERY_HEADS // KV_HEADS
GROUP = 256
ROWS = 64
CHUNKS = 13
KEYS = CHUNKS * ROWS
NDOCS = 64
OWN = 6
FLOW = 7
LAST = 31
MASKED = -1e30


class Place:
    def __init__(self):
        self.w = lax.axis_index("wide")
        self.n = lax.axis_index("narrow")
        self.g = self.w // 2
        self.ylo = self.w % 2
        self.yhi = self.n // 2
        self.c = self.n % 2
        self.across = self.w + 1 - 2 * self.ylo
        self.sibling = self.n + 1 - 2 * self.c


class Exchange:
    def __init__(self, place, win, send_sem, recv_sem, sib_sem):
        self.p = place
        self.win, self.send_sem, self.recv_sem, self.sib_sem = win, send_sem, recv_sem, sib_sem
        self.draining = False

    @staticmethod
    def at(slot):
        return 13 if isinstance(slot, int) and slot == FLOW else 2 * slot

    def chunk(self, s, h, slot):
        return self.win(s, h).at[self.at(slot)]

    def _send(self, cond, s, h, k, src, dst, recv, device):
        def copy():
            return pltpu.make_async_remote_copy(
                src_ref=src, dst_ref=dst, send_sem=self.send_sem.at[s, h, k], recv_sem=recv,
                device_id=device, device_id_type=MESH,
            )

        def go():
            copy().wait_send() if self.draining else copy().start()

        go() if cond is None else pl.when(cond)(go)

    def between(self, s):
        return (self.p.g < LAST, 2) if s == 0 else (self.p.g > 0, -2)

    def put(self, cond, s, h, k, slot, device, to_s, to):
        dst = self.win(to_s, h).at[self.at(to)]
        self._send(cond, s, h, k, self.chunk(s, h, slot), dst, self.recv_sem.at[to_s, h, to], device)

    def onward(self, s, h, slot, cond=None):
        p = self.p
        goes, step = self.between(s)
        goes = goes if cond is None else jnp.logical_and(goes, cond)
        self.put(goes, s, h, 6 - slot, slot, (p.w + step, p.n), s, slot - 4)

    def spread(self, s, h, slot, cond):
        p = self.p
        self.put(cond, s, h, 3, slot, (p.across, p.c), s, 4 + p.yhi)
        self.put(cond, s, h, 4, slot, (p.across, 2 + p.c), s, 3 + p.yhi)

    def fold(self, h):
        p = self.p
        both = jnp.logical_and
        near = both(p.g == LAST - 1, p.ylo == 1)
        here = p.g == LAST
        self.put(near, 0, h, 7, OWN, (p.w + 2, p.n), 1, 0)
        self.put(both(near, p.yhi == 1), 0, h, 8, OWN, (p.w + 2, p.c), 1, 1)
        self.put(here, 0, h, 0, OWN, (p.across, p.n), 1, 2)
        self.put(both(here, p.yhi == 0), 0, h, 1, OWN, (p.across, p.n + 2), 1, 1)
        self.put(both(both(here, p.ylo == 0), p.yhi == 1), 0, h, 1, OWN, (p.w, p.n - 2), 1, 1)
        self.inside(both(here, p.ylo == 0), h, 1, 0)
        for slot in range(3):
            self.inside(p.g == 0, h, 0, slot)

    def share(self, s, h, slot, cond=None):
        if self.draining:
            return
        p = self.p
        if slot == 0:
            cond = p.c == 1 if cond is None else jnp.logical_and(cond, p.c == 1)
        if slot == OWN:
            cond = p.c == 0 if cond is None else jnp.logical_and(cond, p.c == 0)
        at = slot - 1 + p.c
        src, dst = self.chunk(s, h, slot), self.win(s, h).at[2 * at + 1]

        def go():
            pltpu.make_async_remote_copy(
                src_ref=src, dst_ref=dst, send_sem=self.sib_sem.at[0, s, h], recv_sem=self.sib_sem.at[1, s, h],
                device_id=(p.w, p.sibling), device_id_type=MESH,
            ).start()

        go() if cond is None else pl.when(cond)(go)

    def inside(self, cond, h, s, slot):
        if self.draining:
            return
        pl.when(cond)(
            lambda: pltpu.make_async_copy(
                self.chunk(0, h, OWN), self.chunk(s, h, slot), self.recv_sem.at[s, h, slot]
            ).start()
        )

    def await_slot(self, s, h, slot, cond=None):
        if self.draining:
            return
        if cond is not None:
            pl.when(cond)(lambda: self.await_slot(s, h, slot))
            return
        ref = self.chunk(s, h, slot)
        pltpu.make_async_copy(ref, ref, self.recv_sem.at[s, h, slot]).wait()

    def roles(self, s):
        p = self.p
        first = p.ylo == s
        second = p.ylo != s
        low, high = p.yhi == 0, p.yhi == 1
        both = jnp.logical_and
        return first, second, both(first, low), both(first, high), both(second, low), both(second, high)

    def over(self, s, h, k, slot, half, to, cond):
        self.put(cond, s, h, k, slot, (self.p.across, 2 * half + self.p.c), s, to)

    def phase(self, number, s, h):
        p = self.p
        F, S, Fl, Fh, Sl, Sh = self.roles(s)
        low, high = p.yhi == 0, p.yhi == 1
        parity = h % 2
        carrier = jnp.logical_and(F, p.yhi == parity)

        def take(slot, cond=None, on=False):
            self.await_slot(s, h, slot, cond)
            if on:
                self.onward(s, h, slot, cond)

        if number == 0:
            self.onward(s, h, OWN)
            self.spread(s, h, OWN, F)
            self.over(s, h, 5, OWN, parity, FLOW, Sl)
            self.share(s, h, OWN)
            if s == 0:
                self.fold(h)
        elif number == 1:
            take(2)
            self.spread(s, h, 2, S)
            self.share(s, h, 2)
            take(5, Sl, True)
            self.share(s, h, 5, Sl)
            take(4, S, True)
            self.share(s, h, 4, S)
            take(3, Sh)
            self.over(s, h, 5, 3, 1, 5, Sh)
            self.share(s, h, 3, Sh)
            take(FLOW, carrier)
            self.over(s, h, 6, FLOW, 1, 5, carrier)
        elif number == 2:
            take(0, S)
            self.over(s, h, 6, 0, 0, 3, Sh)
            self.share(s, h, 0, S)
            take(1, Sl)
            self.share(s, h, 1, Sl)
            take(5, Fl)
            self.over(s, h, 5, 5, 0, 3, Fl)
            self.onward(s, h, 5, Fl)
            self.share(s, h, 5, Fl)
            take(4, F, True)
            self.share(s, h, 4, F)
            take(3, Fh)
            self.share(s, h, 3, Fh)
            take(5, high, True)
            self.share(s, h, 5, high)
        elif number == 3:
            take(3, low)
            self.share(s, h, 3, low)
            take(0, F)
            self.share(s, h, 0, F)
            rest = jnp.logical_not(Sl)
            take(1, rest)
            self.share(s, h, 1, rest)

    def arrived(self, s, h):
        ref = self.win(s, h).at[0:6]
        for way in (1, 0):
            pltpu.make_async_copy(ref, ref, self.sib_sem.at[way, s, h]).wait()


def greet(p):
    barrier = pltpu.get_barrier_semaphore()

    def signal(device):
        pl.semaphore_signal(barrier, inc=1, device_id=device, device_id_type=MESH)

    def pair(wide):
        signal((wide, p.c))
        signal((wide, 2 + p.c))

    both = jnp.logical_and
    top = p.g // LAST
    below = p.g // (LAST - 1) - top
    up, down = 1 - top, 1 - (LAST - p.g) // LAST
    pair(p.across)
    signal((p.w, p.sibling))
    pl.when(p.g < LAST)(lambda: signal((p.w + 2, p.n)))
    pl.when(p.g > 0)(lambda: signal((p.w - 2, p.n)))
    pl.when(both(p.g == LAST, p.ylo == 0))(lambda: signal((p.w, p.n + 2 - 4 * p.yhi)))
    pl.when(both(both(p.g == LAST - 1, p.ylo == 1), p.yhi == 1))(lambda: signal((p.w + 2, p.c)))
    pl.when(both(both(p.g == LAST, p.ylo == 1), p.yhi == 0))(lambda: signal((p.w - 2, 2 + p.c)))
    turn = p.ylo * (below * p.yhi + top * (1 - p.yhi)) + top * (1 - p.ylo)
    pl.semaphore_wait(barrier, 3 + up + down + turn)


def masks(start, lengths_ref, key_side, query_side):
    lane = lax.broadcasted_iota(jnp.int32, (1, 128), 1)
    begins = jnp.zeros((1, 128), jnp.int32)
    ends = jnp.zeros((1, 128), jnp.int32)
    for e in range(NDOCS):
        length = lengths_ref[e]
        begins = begins + jnp.where(lane > e, length, 0)
        ends = ends + jnp.where(lane >= e, length, 0)
    lanes = lax.broadcasted_iota(jnp.int32, (KEYS, 128), 1)
    place = lax.broadcasted_iota(jnp.int32, (KEYS, 128), 0) - (KEYS - ROWS)
    pos = place + start
    in_doc = ((pos >= begins) & (pos < ends)) | (pos < 0)
    own = place == lanes - NDOCS
    key_side[...] = jnp.where(((lanes < NDOCS) & in_doc) | ((lanes >= NDOCS) & own), 1.0, 0.0).astype(jnp.bfloat16)
    lanes = lax.broadcasted_iota(jnp.int32, (ROWS, 128), 1)
    row = lax.broadcasted_iota(jnp.int32, (ROWS, 128), 0)
    pos = row + start
    other = (pos < begins) | (pos >= ends)
    later = lanes - NDOCS > row
    query_side[...] = jnp.where(((lanes < NDOCS) & other) | (later & (lanes >= NDOCS)), MASKED, 0.0).astype(jnp.bfloat16)


TILE_HEADS = 4
PARTS = ((0, 256), (256, 512), (512, 768), (768, 896))


def attend(q_ref, side_ref, keys_side_ref, win_ref, h, row, write):
    rate = math.log2(math.e) / math.sqrt(HEAD_DIM)
    k = win_ref[:, :, 0:HEAD_DIM].reshape(KEYS, HEAD_DIM)
    v = win_ref[:, :, HEAD_DIM : 2 * HEAD_DIM].reshape(KEYS, HEAD_DIM)
    k = jnp.concatenate([k, keys_side_ref[...]], axis=1)
    v = jnp.concatenate([v, jnp.ones((KEYS, HEAD_DIM), jnp.bfloat16)], axis=1)
    k = jnp.concatenate([k, k[KEYS - ROWS :]], axis=0)
    v = jnp.concatenate([v, jnp.zeros((ROWS, 2 * HEAD_DIM), jnp.bfloat16)], axis=0)
    side = side_ref[...]
    tiles = SHARE // TILE_HEADS

    def columns(a):
        return pl.ds(pl.multiple_of((h * SHARE + a) * HEAD_DIM, HEAD_DIM), HEAD_DIM)

    def queries(t):
        heads = range(t * TILE_HEADS, (t + 1) * TILE_HEADS)
        return jnp.concatenate(
            [jnp.concatenate([q_ref[row : row + ROWS, columns(a)], side], axis=1) for a in heads], axis=0
        )

    def score(q, part):
        low, high = part
        return lax.dot_general(q, k[low:high], (((1,), (1,)), ((), ())), preferred_element_type=jnp.float32)

    q = queries(0)
    ahead = [score(q, part) for part in PARTS]
    for t in range(tiles):
        scores, ahead = ahead, []
        if t + 1 < tiles:
            q = queries(t + 1)
        top = functools.reduce(
            jnp.maximum, [s[:, at : at + 128] for s in scores for at in range(0, s.shape[1], 128)]
        )
        top = jnp.max(top, axis=1, keepdims=True)
        mixed = None
        for part, s in zip(PARTS, scores):
            if t + 1 < tiles:
                ahead.append(score(q, part))
            weights = jnp.exp2((s - top) * rate).astype(jnp.bfloat16)
            new = jnp.dot(weights, v[part[0] : part[1]], preferred_element_type=jnp.float32)
            mixed = new if mixed is None else mixed + new
        mixed = mixed[:, 0:HEAD_DIM] / mixed[:, HEAD_DIM : 2 * HEAD_DIM]
        for i in range(TILE_HEADS):
            write(columns(t * TILE_HEADS + i), mixed[i * ROWS : (i + 1) * ROWS])


def kernel(
    order_hbm, lengths_hbm, q_hbm, k_hbm, v_hbm, out_ref, order_ref, lengths_ref, q_ref, k_ref, v_ref, win, key_side,
    query_side, in_sem, send_sem, recv_sem, sib_sem,
):
    p = Place()
    loads = [
        pltpu.make_async_copy(src, dst, in_sem.at[i])
        for i, (src, dst) in enumerate(
            ((order_hbm, order_ref), (k_hbm, k_ref), (v_hbm, v_ref), (lengths_hbm, lengths_ref), (q_hbm, q_ref))
        )
    ]
    for load in loads:
        load.start()
    greet(p)
    for load in loads[:4]:
        load.wait()
    first = order_ref[0, p.w]

    def swapped(width):
        return jnp.full((ROWS, width), first, jnp.int32) >= 64

    def own(h):
        cols = pl.ds(pl.multiple_of(h * HEAD_DIM, HEAD_DIM), HEAD_DIM)
        other = swapped(HEAD_DIM)
        for part, ref in enumerate((k_ref, v_ref)):
            low, high = ref[0:ROWS, cols], ref[ROWS : 2 * ROWS, cols]
            to = slice(part * HEAD_DIM, (part + 1) * HEAD_DIM)
            win[0, h, 12, :, to] = jnp.where(other, high, low)
            win[1, h, 12, :, to] = jnp.where(other, low, high)
        for s in range(2):
            ex.phase(0, s, h)

    ex = Exchange(p, lambda s, h: win.at[s, h], send_sem, recv_sem, sib_sem)

    def turn_queries(i, carry):
        wide = 1024
        cols = pl.ds(pl.multiple_of(i * wide, wide), wide)
        low, high = q_ref[0:ROWS, cols], q_ref[ROWS : 2 * ROWS, cols]
        other = swapped(wide)
        q_ref[0:ROWS, cols] = jnp.where(other, high, low)
        q_ref[ROWS : 2 * ROWS, cols] = jnp.where(other, low, high)
        return carry

    def late_rows(cols, mixed):
        out_ref[ROWS : 2 * ROWS, cols] = mixed

    def early_rows(cols, mixed):
        late = out_ref[ROWS : 2 * ROWS, cols]
        other = swapped(HEAD_DIM)
        out_ref[0:ROWS, cols] = jnp.where(other, late, mixed)
        out_ref[ROWS : 2 * ROWS, cols] = jnp.where(other, mixed, late)

    def unit(s, h):
        ex.arrived(s, h)
        write = late_rows if s == 1 else early_rows
        attend(q_ref, query_side.at[s], key_side.at[s], win.at[s, h, 0:CHUNKS], h, s * ROWS, write)

    def both(number, h):
        for s in range(2):
            ex.phase(number, s, h)

    def fill(t, carry):
        own(t)

        @pl.when(t == 0)
        def _():
            masks(p.w * GROUP + p.n * ROWS, lengths_ref, key_side.at[0], query_side.at[0])
            masks((2 * 64 - 1 - p.w) * GROUP + p.n * ROWS, lengths_ref, key_side.at[1], query_side.at[1])

        @pl.when(t == 1)
        def _():
            loads[4].wait()
            lax.fori_loop(0, 8, turn_queries, 0)

        for number in range(1, 4):
            pl.when(t >= number)(lambda number=number: both(number, t - number))
        return carry

    def work(h, carry):
        pl.when(h + 3 < KV_HEADS)(lambda: both(1, h + 3))
        unit(1, h)
        for number, later in ((2, 2), (3, 1)):
            pl.when(h + later < KV_HEADS)(lambda number=number, later=later: both(number, h + later))
        unit(0, h)
        return carry

    lax.fori_loop(0, KV_HEADS, fill, 0)
    lax.fori_loop(0, KV_HEADS, work, 0)
    ex.draining = True

    def drain(h, carry):
        for number in range(3):
            both(number, h)
        return carry

    lax.fori_loop(0, KV_HEADS, drain, 0)


def attention(block_order, doc_lengths, queries, keys, values):
    held = pl.BlockSpec(memory_space=pltpu.HBM)
    flops = 2 * 2 * ROWS * QUERY_HEADS * KEYS * 512
    operands = [
        pltpu.with_memory_space_constraint(a, pltpu.HBM) for a in (block_order, doc_lengths, queries, keys, values)
    ]
    return pl.pallas_call(
        kernel,
        out_shape=pltpu.VMEM(queries.shape, jnp.float32),
        in_specs=[held] * 5,
        out_specs=pl.BlockSpec(memory_space=pltpu.VMEM),
        scratch_shapes=[
            pltpu.SMEM((2, 64), jnp.int32),
            pltpu.SMEM((NDOCS,), jnp.int32),
            pltpu.VMEM((2 * ROWS, QUERY_HEADS * HEAD_DIM), jnp.bfloat16),
            pltpu.VMEM((2 * ROWS, KV_HEADS * HEAD_DIM), jnp.bfloat16),
            pltpu.VMEM((2 * ROWS, KV_HEADS * HEAD_DIM), jnp.bfloat16),
            pltpu.VMEM((2, KV_HEADS, CHUNKS + 1, ROWS, 2 * HEAD_DIM), jnp.bfloat16),
            pltpu.VMEM((2, KEYS, HEAD_DIM), jnp.bfloat16),
            pltpu.VMEM((2, ROWS, HEAD_DIM), jnp.bfloat16),
            pltpu.SemaphoreType.DMA((5,)),
            pltpu.SemaphoreType.DMA((2, KV_HEADS, 9)),
            pltpu.SemaphoreType.DMA((2, KV_HEADS, 8)),
            pltpu.SemaphoreType.DMA((2, 2, KV_HEADS)),
        ],
        compiler_params=pltpu.CompilerParams(collective_id=0, has_side_effects=True, vmem_limit_bytes=40 << 20),
        cost_estimate=pl.CostEstimate(flops=flops, bytes_accessed=10 << 20, transcendentals=0),
        name="exchange_attend",
    )(*operands)


def body(queries, keys, values, block_order, doc_lengths):
    return attention(block_order.T, doc_lengths, queries, keys, values)


def solution(mesh):
    rows = P(("wide", "narrow"), None)
    return jax.shard_map(
        body, mesh=mesh, in_specs=(rows, rows, rows, P(), P()), out_specs=rows, check_vma=False
    )
```

time: 245 us -> 37.2 us (0.15)
  waiting for transfers between devices: 74.6 us -> 0 us
  local copies, waits for them, and re-layouts: 51.5 us -> 2.02 us
  between operations: 40.2 us -> 0.01 us
  Pallas kernels: 0 us -> 35 us
  starting transfers between devices: 30.4 us -> 0 us
  matrix products: 29 us -> 0 us
  other arithmetic: 17 us -> 0 us
    ppermute x6 -> x0, waiting for transfers between devices: 47.4 us -> none  [from_behind(): return lax.ppermute(block, axis, route)]
    pallas_call x0 -> x1, Pallas kernels: none -> 35 us  [attention(): pl.pallas_call(kernel, out_shape=pltpu.VMEM(queries.shape, jnp.float32),...]
    ppermute x6 -> x0, starting transfers between devices: 30.4 us -> none  [from_behind(): return lax.ppermute(block, axis, route)]
    dot_general x10 -> x0, matrix products: 29 us -> none  [the longest x2 16.3 us: attend(): jnp.einsum('hgqk,khd->hgqd', rounded, all_values, preferred_element_type=...]
    all_gather x1 -> x0, waiting for transfers between devices: 27.2 us -> none  [body(): kv_whole = lax.all_gather(kv_local, 'narrow', axis=1, tiled=True)]
    dynamic_slice x18 -> x0, local copies, waits for them, and re-layouts: 24.7 us -> none  [the longest x8 14.3 us: attend(): candidates[offset_id, 0, slot_id].reshape(group_rows, KV_HEADS, HEAD_DIM)]
    another operation x10 -> x0, local copies, waits for them, and re-layouts: 11.7 us -> none  [the longest x8 11.6 us: attend(): candidates[offset_id, 1, slot_id].reshape(group_rows, KV_HEADS, HEAD_DIM)]
    reduce_sum x5 -> x0, other arithmetic: 9.7 us -> none  [the longest x2 6.56 us: attend(): weight_sum = jnp.sum(weights, axis=-1, keepdims=True)]
  transfers between devices with their start and end apart: 7 -> 0, of which waited for: 4 -> 0; matrix products, arithmetic and copies ran while one was open for 6% -> 0% of each run, Pallas kernels for 0% -> 0%
where the time goes in v1:
time: 37.2 us; the launch traced here: 37.1 us
  Pallas kernels  35 us (94%)
  local copies, waits for them, and re-layouts  2.02 us (5%)
    pallas_call x1, Pallas kernels, attention(): pl.pallas_call(kernel, out_shape=pltpu.VMEM(queries.shape, jnp.float32),...  35 us
    unnamed x1, local copies, waits for them, and re-layouts  2.02 us

profile of v1, /device:TPU:6, one launch (start us, length us, event | category | flops | bytes accessed | tf_op | source)
XLA Modules:
  0.0 37.1 jit_solution(2803073238722820214)
XLA Ops:
  0.0 35.0 %exchange_attend.1 = f32[128,8192]{1,0:T(8,128)S(1)} custom-call(s32[2,64]{1,0:T(2,128)} %bitcast.1, s32[64]{0:T(128)} %lengths_hbm.1, bf16[128,8192]{1,0:T(8,128)(2,1)} %q_hbm.1, bf16[128,512]{1,0:T(8,128)(2,1)} %k_hbm.1, bf16[128,512]{1,0:T(8,128)(2,1)} %v_hbm.1), custom_call_target="tpu_custom_call" | custom-call | flops 6979321856 | bytes 10485760 | tf_op jit(solution)/shard_map/exchange_attend/pallas_call | solution.py:408
  35.1 2.0 %copy.7 = f32[128,8192]{1,0:T(8,128)} copy(f32[128,8192]{1,0:T(8,128)S(1)} %exchange_attend.1) | data formatting | bytes 8388608

commit v2 on v1

--- a/solution.py
+++ b/solution.py
@@ -298,12 +298,12 @@
             mixed = new if mixed is None else mixed + new
         mixed = mixed[:, 0:HEAD_DIM] / mixed[:, HEAD_DIM : 2 * HEAD_DIM]
         for i in range(TILE_HEADS):
-            write(columns(t * TILE_HEADS + i), mixed[i * ROWS : (i + 1) * ROWS])
+            write(t * TILE_HEADS + i, mixed[i * ROWS : (i + 1) * ROWS])
 
 
 def kernel(
-    order_hbm, lengths_hbm, q_hbm, k_hbm, v_hbm, out_ref, order_ref, lengths_ref, q_ref, k_ref, v_ref, win, key_side,
-    query_side, in_sem, send_sem, recv_sem, sib_sem,
+    order_hbm, lengths_hbm, q_hbm, k_hbm, v_hbm, out_ref, win, q_ref, key_side, query_side, order_ref, lengths_ref, k_ref,
+    v_ref, in_sem, send_sem, recv_sem, sib_sem,
 ):
     p = Place()
     loads = [
@@ -344,18 +344,12 @@
         q_ref[ROWS : 2 * ROWS, cols] = jnp.where(other, low, high)
         return carry
 
-    def late_rows(cols, mixed):
-        out_ref[ROWS : 2 * ROWS, cols] = mixed
-
-    def early_rows(cols, mixed):
-        late = out_ref[ROWS : 2 * ROWS, cols]
-        other = swapped(HEAD_DIM)
-        out_ref[0:ROWS, cols] = jnp.where(other, late, mixed)
-        out_ref[ROWS : 2 * ROWS, cols] = jnp.where(other, mixed, late)
-
     def unit(s, h):
+        def write(a, mixed):
+            cols = pl.ds(pl.multiple_of((h * SHARE + a) * HEAD_DIM, HEAD_DIM), HEAD_DIM)
+            out_ref[s, :, cols] = mixed
+
         ex.arrived(s, h)
-        write = late_rows if s == 1 else early_rows
         attend(q_ref, query_side.at[s], key_side.at[s], win.at[s, h, 0:CHUNKS], h, s * ROWS, write)
 
     def both(number, h):
@@ -388,7 +382,9 @@
         return carry
 
     lax.fori_loop(0, KV_HEADS, fill, 0)
-    lax.fori_loop(0, KV_HEADS, work, 0)
+    lax.fori_loop(0, KV_HEADS - 1, work, 0)
+    for s in range(2):
+        ex.arrived(s, KV_HEADS - 1)
     ex.draining = True
 
     def drain(h, carry):
@@ -399,35 +395,84 @@
     lax.fori_loop(0, KV_HEADS, drain, 0)
 
 
+def last_kernel(order_hbm, part_ref, win, q_ref, key_side, query_side, out_hbm, order_ref, o_ref, in_sem, out_sem):
+    load = pltpu.make_async_copy(order_hbm, order_ref, in_sem)
+    load.start()
+    width = SHARE * HEAD_DIM
+    done = (KV_HEADS - 1) * width
+    w = lax.axis_index("wide")
+
+    def unit(s):
+        def write(a, mixed):
+            o_ref[s, :, a * HEAD_DIM : (a + 1) * HEAD_DIM] = mixed
+
+        attend(
+            q_ref, query_side.at[s], key_side.at[s], win.at[s, KV_HEADS - 1, 0:CHUNKS], KV_HEADS - 1, s * ROWS, write
+        )
+
+    unit(1)
+    load.wait()
+    flip = (order_ref[0, w] >= 64).astype(jnp.int32)
+    rows = [pl.ds(pl.multiple_of(at * ROWS, ROWS), ROWS) for at in (flip, 1 - flip)]
+    copies = [
+        pltpu.make_async_copy(part_ref.at[s], out_hbm.at[rows[s], 0:done], out_sem.at[s]) for s in range(2)
+    ] + [pltpu.make_async_copy(o_ref.at[s], out_hbm.at[rows[s], done : done + width], out_sem.at[2 + s]) for s in range(2)]
+    for i in (3, 1, 0):
+        copies[i].start()
+    unit(0)
+    copies[2].start()
+    for copy in copies:
+        copy.wait()
+
+
 def attention(block_order, doc_lengths, queries, keys, values):
     held = pl.BlockSpec(memory_space=pltpu.HBM)
-    flops = 2 * 2 * ROWS * QUERY_HEADS * KEYS * 512
+    near = pl.BlockSpec(memory_space=pltpu.VMEM)
+    width = SHARE * HEAD_DIM
+    flops = 2 * ROWS * SHARE * KEYS * 512
     operands = [
         pltpu.with_memory_space_constraint(a, pltpu.HBM) for a in (block_order, doc_lengths, queries, keys, values)
     ]
-    return pl.pallas_call(
+    parts = pl.pallas_call(
         kernel,
-        out_shape=pltpu.VMEM(queries.shape, jnp.float32),
+        out_shape=(
+            pltpu.VMEM((2, ROWS, (KV_HEADS - 1) * width), jnp.float32),
+            pltpu.VMEM((2, KV_HEADS, CHUNKS + 1, ROWS, 2 * HEAD_DIM), jnp.bfloat16),
+            pltpu.VMEM(queries.shape, jnp.bfloat16),
+            pltpu.VMEM((2, KEYS, HEAD_DIM), jnp.bfloat16),
+            pltpu.VMEM((2, ROWS, HEAD_DIM), jnp.bfloat16),
+        ),
         in_specs=[held] * 5,
-        out_specs=pl.BlockSpec(memory_space=pltpu.VMEM),
+        out_specs=(near,) * 5,
         scratch_shapes=[
             pltpu.SMEM((2, 64), jnp.int32),
             pltpu.SMEM((NDOCS,), jnp.int32),
-            pltpu.VMEM((2 * ROWS, QUERY_HEADS * HEAD_DIM), jnp.bfloat16),
             pltpu.VMEM((2 * ROWS, KV_HEADS * HEAD_DIM), jnp.bfloat16),
             pltpu.VMEM((2 * ROWS, KV_HEADS * HEAD_DIM), jnp.bfloat16),
-            pltpu.VMEM((2, KV_HEADS, CHUNKS + 1, ROWS, 2 * HEAD_DIM), jnp.bfloat16),
-            pltpu.VMEM((2, KEYS, HEAD_DIM), jnp.bfloat16),
-            pltpu.VMEM((2, ROWS, HEAD_DIM), jnp.bfloat16),
             pltpu.SemaphoreType.DMA((5,)),
             pltpu.SemaphoreType.DMA((2, KV_HEADS, 9)),
             pltpu.SemaphoreType.DMA((2, KV_HEADS, 8)),
             pltpu.SemaphoreType.DMA((2, 2, KV_HEADS)),
         ],
-        compiler_params=pltpu.CompilerParams(collective_id=0, has_side_effects=True, vmem_limit_bytes=40 << 20),
-        cost_estimate=pl.CostEstimate(flops=flops, bytes_accessed=10 << 20, transcendentals=0),
+        compiler_params=pltpu.CompilerParams(collective_id=0, has_side_effects=True, vmem_limit_bytes=32 << 20),
+        cost_estimate=pl.CostEstimate(flops=6 * flops, bytes_accessed=4 << 20, transcendentals=0),
         name="exchange_attend",
     )(*operands)
+    return pl.pallas_call(
+        last_kernel,
+        out_shape=jax.ShapeDtypeStruct(queries.shape, jnp.float32),
+        in_specs=[held] + [near] * 5,
+        out_specs=held,
+        scratch_shapes=[
+            pltpu.SMEM((2, 64), jnp.int32),
+            pltpu.VMEM((2, ROWS, width), jnp.float32),
+            pltpu.SemaphoreType.DMA,
+            pltpu.SemaphoreType.DMA((4,)),
+        ],
+        compiler_params=pltpu.CompilerParams(vmem_limit_bytes=32 << 20),
+        cost_estimate=pl.CostEstimate(flops=2 * flops, bytes_accessed=4 << 20, transcendentals=0),
+        name="attend_last",
+    )(operands[0], *parts)
 
 
 def body(queries, keys, values, block_order, doc_lengths):

time: 37.2 us -> 36.3 us (0.976)
  local copies, waits for them, and re-layouts: 2.02 us -> 0 us
  Pallas kernels: 35 us -> 36.2 us
    unnamed x1 -> x0, local copies, waits for them, and re-layouts: 2.02 us -> none
    pallas_call x1 -> x2, Pallas kernels: 35 us -> 36.2 us  [the longest x1 31.9 us: attention(): pl.pallas_call(kernel, out_shape=(pltpu.VMEM((2, ROWS, (KV_HEADS - 1) * w...]
where the time goes in v2:
time: 36.3 us; the launch traced here: 36.2 us
  Pallas kernels  36.2 us (100%)
    pallas_call x1, Pallas kernels, attention(): pl.pallas_call(kernel, out_shape=(pltpu.VMEM((2, ROWS, (KV_HEADS - 1) * w...  31.9 us
    pallas_call x1, Pallas kernels, attention(): pl.pallas_call(last_kernel, out_shape=jax.ShapeDtypeStruct(queries.shape,...  4.36 us

profile of v2, /device:TPU:6, one launch (start us, length us, event | category | flops | bytes accessed | tf_op | source)
XLA Modules:
  0.0 36.2 jit_solution(790124415115034494)
XLA Ops:
  0.0 31.9 %exchange_attend.1 = (f32[2,64,6144]{2,1,0:T(8,128)S(1)}, bf16[2,4,14,64,256]{4,3,2,1,0:T(8,128)(2,1)S(1)}, bf16[128,8192]{1,0:T(8,128)(2,1)S(1)}, bf16[2,832,12...) custom-call(s32[2,64]{1,0:T(2,128)} %bitcast.1, s32[64]{0:T(128)} %lengths_hbm.1, bf16[128,8192]{1,0:T(8,128)(2,1)} %q_hbm.1, ...), custom_call_target="tpu_custom_call" | custom-call | flops 5234491392 | bytes 4194304 | tf_op jit(solution)/shard_map/exchange_attend/pallas_call | solution.py:436
  31.9 4.4 %attend_last.1 = f32[128,8192]{1,0:T(8,128)} custom-call(s32[2,64]{1,0:T(2,128)} %bitcast.2, f32[2,64,6144]{2,1,0:T(8,128)S(1)} %get-tuple-element.10.part_ref, bf16[2,4,14,64,256]{4,3,2,1,0:T(8,128)(2,1)S(1)} %get-tuple-element.11.win, bf16[128,8192]{1,0:T(8,128)(2,1)S(1)} %get-tuple-element.12.q_ref, bf16[2,832,128]{2,1,0:T(8,128)(2,1)S(1)} %get-tuple-element.13.key_side, ...), custom_call_target="tpu_custom_call" | custom-call | flops 1744830464 | bytes 4194304 | tf_op jit(solution)/shard_map/attend_last/pallas_call | solution.py:461

commit v3 on v2

v3 whole, which is shorter than its diff:
```python
import functools
import math

import jax
import jax.numpy as jnp
from jax import lax
from jax.experimental import pallas as pl
from jax.experimental.pallas import tpu as pltpu
from jax.sharding import PartitionSpec as P

MESH = pl.DeviceIdType.MESH
QUERY_HEADS = 64
KV_HEADS = 4
HEAD_DIM = 128
SHARE = QUERY_HEADS // KV_HEADS
GROUP = 256
ROWS = 64
CHUNKS = 13
KEYS = CHUNKS * ROWS
NDOCS = 64
FIRST_HEADS = KV_HEADS - 1
OWN = 6
FLOW = 7
LAST = 31
MASKED = -1e30


class Place:
    def __init__(self):
        self.w = lax.axis_index("wide")
        self.n = lax.axis_index("narrow")
        self.g = self.w // 2
        self.ylo = self.w % 2
        self.yhi = self.n // 2
        self.c = self.n % 2
        self.across = self.w + 1 - 2 * self.ylo
        self.sibling = self.n + 1 - 2 * self.c


class Exchange:
    def __init__(self, place, win, send_sem, recv_sem, sib_sem):
        self.p = place
        self.win, self.send_sem, self.recv_sem, self.sib_sem = win, send_sem, recv_sem, sib_sem

    def chunk(self, s, h, slot):
        return self.win(s, h).at[OWN, 1] if isinstance(slot, int) and slot == FLOW else self.win(s, h).at[slot, 0]

    def put(self, s, h, k, slot, device, to_s, to):
        pltpu.make_async_remote_copy(
            src_ref=self.chunk(s, h, slot), dst_ref=self.chunk(to_s, h, to), send_sem=self.send_sem.at[s, h, k],
            recv_sem=self.recv_sem.at[to_s, h, to], device_id=device, device_id_type=MESH,
        ).start()

    def goes(self, s):
        return self.p.g < LAST if s == 0 else self.p.g > 0

    def onward(self, s, h, *slots):
        p = self.p
        step = 2 if s == 0 else -2

        def go():
            for slot in slots:
                self.put(s, h, 0, slot, (p.w + step, p.n), s, slot - 4)

        pl.when(self.goes(s))(go)

    def spread(self, s, h, slot):
        p = self.p
        self.put(s, h, 1, slot, (p.across, p.c), s, 4 + p.yhi)
        self.put(s, h, 1, slot, (p.across, 2 + p.c), s, 3 + p.yhi)

    def over(self, s, h, k, slot, half, to):
        self.put(s, h, k, slot, (self.p.across, 2 * half + self.p.c), s, to)

    def folds(self):
        p = self.p
        both = jnp.logical_and
        near = both(p.g == LAST - 1, p.ylo == 1)
        here = p.g == LAST
        return (
            (near, 4, (p.w + 2, p.n), 0),
            (both(near, p.yhi == 1), 5, (p.w + 2, p.c), 1),
            (here, 6, (p.across, p.n), 2),
            (both(here, p.yhi == 0), 7, (p.across, p.n + 2), 1),
            (both(both(here, p.ylo == 0), p.yhi == 1), 8, (p.w, p.n - 2), 1),
        )

    def inside(self, h, s, slot):
        pltpu.make_async_copy(
            self.chunk(0, h, OWN), self.chunk(s, h, slot), self.recv_sem.at[s, h, slot]
        ).start()

    def ends(self, h):
        p = self.p
        for cond, k, device, to in self.folds():
            pl.when(cond)(lambda k=k, device=device, to=to: self.put(0, h, k, OWN, device, 1, to))
        pl.when(jnp.logical_and(p.g == LAST, p.ylo == 0))(lambda: self.inside(h, 1, 0))

        @pl.when(p.g == 0)
        def _():
            for slot in range(3):
                self.inside(h, 0, slot)

    def take(self, s, h, *slots):
        for slot in slots:
            ref = self.chunk(s, h, slot)
            pltpu.make_async_copy(ref, ref, self.recv_sem.at[s, h, slot]).wait()

    def role(self, s):
        p = self.p
        return 2 * (p.ylo if s == 0 else 1 - p.ylo) + p.yhi

    def carries(self, s, h):
        return self.role(s) == h % 2

    def phase(self, number, s, h):
        p = self.p
        role = self.role(s)
        parity = h % 2

        def flow():
            self.take(s, h, FLOW)
            self.over(s, h, 3, FLOW, 1, 5)

        def share(low, high):
            to = low - (1 if high == 7 or low == 1 else 0)
            pltpu.make_async_remote_copy(
                src_ref=self.win(s, h).at[low:high, 0], dst_ref=self.win(s, h).at[to : to + high - low, 1],
                send_sem=self.sib_sem.at[0, s, h], recv_sem=self.sib_sem.at[1, s, h],
                device_id=(p.w, p.sibling), device_id_type=MESH,
            ).start()

        if number == 0:
            self.onward(s, h, OWN)
            pl.when(role < 2)(lambda: self.spread(s, h, OWN))
            pl.when(role == 2)(lambda: self.over(s, h, 2, OWN, parity, FLOW))
            if s == 0:
                pl.when(jnp.logical_or(p.g == 0, p.g >= LAST - 1))(lambda: self.ends(h))
        elif number == 1:
            pl.when(role == parity)(flow)

            @pl.when(role == 2)
            def _():
                self.take(s, h, 5, 4)
                self.onward(s, h, 5, 4)

            @pl.when(role == 3)
            def _():
                self.take(s, h, 4, 3)
                self.onward(s, h, 4)
                self.over(s, h, 2, 3, 1, 5)

        elif number == 2:
            self.take(s, h, 2)
            pl.when(role >= 2)(lambda: self.spread(s, h, 2))

        elif number == 3:

            @pl.when(role == 0)
            def _():
                self.take(s, h, 5)
                self.over(s, h, 2, 5, 0, 3)
                self.take(s, h, 4)
                self.onward(s, h, 5, 4)

            @pl.when(role == 1)
            def _():
                self.take(s, h, 4, 3, 5)
                self.onward(s, h, 4, 5)

            pl.when(role == 2)(lambda: self.take(s, h, 0, 1))

            @pl.when(role == 3)
            def _():
                self.take(s, h, 0)
                self.over(s, h, 3, 0, 0, 3)
                self.take(s, h, 5)
                self.onward(s, h, 5)

            pl.when(p.c == 0)(lambda: share(4, 7))
            pl.when(p.c == 1)(lambda: share(4, 6))

        elif number == 4:
            pl.when(role == 0)(lambda: self.take(s, h, 3, 0, 1))
            pl.when(role == 1)(lambda: self.take(s, h, 0, 1))
            pl.when(role == 2)(lambda: self.take(s, h, 3))
            pl.when(role == 3)(lambda: self.take(s, h, 1))
            pl.when(p.c == 0)(lambda: share(1, 4))
            pl.when(p.c == 1)(lambda: share(0, 4))

    def arrived(self, s, h):
        ref = self.win(s, h).at[0:6, 1]
        for way in (1, 0):
            pltpu.make_async_copy(ref, ref, self.sib_sem.at[way, s, h]).wait()

    def drain(self, h):
        p = self.p
        for s in range(2):
            role = self.role(s)

            def sent(k, count, s=s):
                ref = self.win(s, h).at[0:count, 0]
                pltpu.make_async_copy(ref, ref, self.send_sem.at[s, h, k]).wait()

            pl.when(self.goes(s))(lambda sent=sent: sent(0, 3))
            sent(1, 2)
            pl.when(role != 1)(lambda sent=sent: sent(2, 1))
            pl.when(jnp.logical_or(role == 3, role == h % 2))(lambda sent=sent: sent(3, 1))

            if s == 0:

                @pl.when(p.g >= LAST - 1)
                def _(sent=sent):
                    for cond, k, _, _ in self.folds():
                        pl.when(cond)(lambda k=k: sent(k, 1))


def greet(p):
    barrier = pltpu.get_barrier_semaphore()

    def signal(device):
        pl.semaphore_signal(barrier, inc=1, device_id=device, device_id_type=MESH)

    def pair(wide):
        signal((wide, p.c))
        signal((wide, 2 + p.c))

    both = jnp.logical_and
    top = p.g // LAST
    below = p.g // (LAST - 1) - top
    up, down = 1 - top, 1 - (LAST - p.g) // LAST
    pair(p.across)
    signal((p.w, p.sibling))
    pl.when(p.g < LAST)(lambda: signal((p.w + 2, p.n)))
    pl.when(p.g > 0)(lambda: signal((p.w - 2, p.n)))
    pl.when(both(p.g == LAST, p.ylo == 0))(lambda: signal((p.w, p.n + 2 - 4 * p.yhi)))
    pl.when(both(both(p.g == LAST - 1, p.ylo == 1), p.yhi == 1))(lambda: signal((p.w + 2, p.c)))
    pl.when(both(both(p.g == LAST, p.ylo == 1), p.yhi == 0))(lambda: signal((p.w - 2, 2 + p.c)))
    turn = p.ylo * (below * p.yhi + top * (1 - p.yhi)) + top * (1 - p.ylo)
    pl.semaphore_wait(barrier, 3 + up + down + turn)


def masks(start, lengths_ref, key_side, query_side, reach):
    lane = lax.broadcasted_iota(jnp.int32, (1, 128), 1)
    begins = jnp.zeros((1, 128), jnp.int32)
    ends = jnp.zeros((1, 128), jnp.int32)
    for e in range(NDOCS):
        length = lengths_ref[e]
        begins = begins + jnp.where(lane > e, length, 0)
        ends = ends + jnp.where(lane >= e, length, 0)
    back = jnp.where(begins <= start, begins, 0) - (start - (KEYS - ROWS))
    reach[...] = jnp.broadcast_to(back, (8, 128)).astype(jnp.float32)
    lanes = lax.broadcasted_iota(jnp.int32, (KEYS, 128), 1)
    place = lax.broadcasted_iota(jnp.int32, (KEYS, 128), 0) - (KEYS - ROWS)
    pos = place + start
    in_doc = ((pos >= begins) & (pos < ends)) | (pos < 0)
    own = place == lanes - NDOCS
    key_side[...] = jnp.where(((lanes < NDOCS) & in_doc) | ((lanes >= NDOCS) & own), 1.0, 0.0).astype(jnp.bfloat16)
    lanes = lax.broadcasted_iota(jnp.int32, (ROWS, 128), 1)
    row = lax.broadcasted_iota(jnp.int32, (ROWS, 128), 0)
    pos = row + start
    other = (pos < begins) | (pos >= ends)
    later = lanes - NDOCS > row
    query_side[...] = jnp.where(((lanes < NDOCS) & other) | (later & (lanes >= NDOCS)), MASKED, 0.0).astype(jnp.bfloat16)


TILE_HEADS = 4
PARTS = ((0, 256), (256, 512), (512, 768), (768, 896))


def attend(q_ref, side_ref, keys_side_ref, win_ref, h, row, write, base=0):
    rate = math.log2(math.e) / math.sqrt(HEAD_DIM)
    k, v = [
        jnp.concatenate(
            [win_ref[0:OWN, :, :, cols].reshape(KEYS - ROWS, HEAD_DIM), win_ref[OWN, 0, :, cols]], axis=0
        )
        for cols in (slice(0, HEAD_DIM), slice(HEAD_DIM, 2 * HEAD_DIM))
    ]
    k = jnp.concatenate([k, keys_side_ref[...]], axis=1)
    v = jnp.concatenate([v, jnp.ones((KEYS, HEAD_DIM), jnp.bfloat16)], axis=1)
    if base:
        k, v = k[base:], v[base:]
        parts = [(at, at + 256) for at in range(0, KEYS - base, 256)]
    else:
        k = jnp.concatenate([k, k[KEYS - ROWS :]], axis=0)
        v = jnp.concatenate([v, jnp.zeros((ROWS, 2 * HEAD_DIM), jnp.bfloat16)], axis=0)
        parts = PARTS
    side = side_ref[...]
    tiles = SHARE // TILE_HEADS

    def columns(a):
        return pl.ds(pl.multiple_of((h * SHARE + a) * HEAD_DIM, HEAD_DIM), HEAD_DIM)

    def queries(t):
        heads = range(t * TILE_HEADS, (t + 1) * TILE_HEADS)
        return jnp.concatenate(
            [jnp.concatenate([q_ref[row : row + ROWS, columns(a)], side], axis=1) for a in heads], axis=0
        )

    def score(q, part):
        low, high = part
        return lax.dot_general(q, k[low:high], (((1,), (1,)), ((), ())), preferred_element_type=jnp.float32)

    q = queries(0)
    ahead = [score(q, part) for part in parts]
    for t in range(tiles):
        scores, ahead = ahead, []
        if t + 1 < tiles:
            q = queries(t + 1)
        top = functools.reduce(
            jnp.maximum, [s[:, at : at + 128] for s in scores for at in range(0, s.shape[1], 128)]
        )
        top = jnp.max(top, axis=1, keepdims=True)
        mixed = None
        for part, s in zip(parts, scores):
            if t + 1 < tiles:
                ahead.append(score(q, part))
            weights = jnp.exp2((s - top) * rate).astype(jnp.bfloat16)
            new = jnp.dot(weights, v[part[0] : part[1]], preferred_element_type=jnp.float32)
            mixed = new if mixed is None else mixed + new
        mixed = mixed[:, 0:HEAD_DIM] / mixed[:, HEAD_DIM : 2 * HEAD_DIM]
        for i in range(TILE_HEADS):
            write(t * TILE_HEADS + i, mixed[i * ROWS : (i + 1) * ROWS])


def kernel(
    order_hbm, lengths_hbm, q_hbm, k_hbm, v_hbm, out_ref, win, q_ref, key_side, query_side, reach, order_ref, lengths_ref,
    k_ref, v_ref, in_sem, send_sem, recv_sem, sib_sem,
):
    p = Place()
    loads = [
        pltpu.make_async_copy(src, dst, in_sem.at[i])
        for i, (src, dst) in enumerate(
            ((order_hbm, order_ref), (k_hbm, k_ref), (v_hbm, v_ref), (lengths_hbm, lengths_ref), (q_hbm, q_ref))
        )
    ]
    for load in loads:
        load.start()
    greet(p)
    for load in loads[:4]:
        load.wait()
    first = order_ref[0, p.w]
    reach[2] = jnp.full((8, 128), first, jnp.int32).astype(jnp.float32)

    def swapped(width):
        return jnp.full((ROWS, width), first, jnp.int32) >= 64

    def own(h):
        cols = pl.ds(pl.multiple_of(h * HEAD_DIM, HEAD_DIM), HEAD_DIM)
        other = swapped(HEAD_DIM)
        for part, ref in enumerate((k_ref, v_ref)):
            low, high = ref[0:ROWS, cols], ref[ROWS : 2 * ROWS, cols]
            to = slice(part * HEAD_DIM, (part + 1) * HEAD_DIM)
            win[0, h, OWN, 0, :, to] = jnp.where(other, high, low)
            win[1, h, OWN, 0, :, to] = jnp.where(other, low, high)
        for s in range(2):
            ex.phase(0, s, h)

    ex = Exchange(p, lambda s, h: win.at[s, h], send_sem, recv_sem, sib_sem)

    def turn_queries(i, carry):
        wide = 1024
        cols = pl.ds(pl.multiple_of(i * wide, wide), wide)
        low, high = q_ref[0:ROWS, cols], q_ref[ROWS : 2 * ROWS, cols]
        other = swapped(wide)
        q_ref[0:ROWS, cols] = jnp.where(other, high, low)
        q_ref[ROWS : 2 * ROWS, cols] = jnp.where(other, low, high)
        return carry

    def unit(s, h):
        def write(a, mixed):
            cols = pl.ds(pl.multiple_of((h * SHARE + a) * HEAD_DIM, HEAD_DIM), HEAD_DIM)
            out_ref[s, :, cols] = mixed

        ex.arrived(s, h)
        attend(q_ref, query_side.at[s], key_side.at[s], win.at[s, h], h, s * ROWS, write)

    def at(h, heads, do):
        pl.when(jnp.logical_and(h >= 0, h < heads))(lambda: do(h))

    def step(t, carry):
        def relay(number, s, later):
            at(t - later, KV_HEADS, lambda h: ex.phase(number, s, h))

        at(t, KV_HEADS, own)

        @pl.when(t == 0)
        def _():
            masks(p.w * GROUP + p.n * ROWS, lengths_ref, key_side.at[0], query_side.at[0], reach.at[0])
            masks((2 * 64 - 1 - p.w) * GROUP + p.n * ROWS, lengths_ref, key_side.at[1], query_side.at[1], reach.at[1])

        @pl.when(t == 1)
        def _():
            loads[4].wait()
            lax.fori_loop(0, 8, turn_queries, 0)

        relay(1, 0, 1)
        relay(1, 1, 1)
        relay(2, 1, 1)
        relay(2, 0, 1)
        at(t - KV_HEADS, FIRST_HEADS, lambda h: unit(1, h))
        relay(3, 1, 2)
        relay(3, 0, 2)
        relay(4, 1, 3)
        relay(4, 0, 3)
        at(t - KV_HEADS, FIRST_HEADS, lambda h: unit(0, h))
        at(t - KV_HEADS, KV_HEADS, ex.drain)
        return carry

    lax.fori_loop(0, 2 * KV_HEADS, step, 0)
    for s in range(2):
        ex.arrived(s, FIRST_HEADS)


def last_kernel(part_ref, win, q_ref, key_side, query_side, reach, out_hbm, o_ref, part_sem, out_sem):
    width = SHARE * HEAD_DIM
    flip = (jnp.max(reach[2]) >= 64).astype(jnp.int32)
    rows = [pl.ds(pl.multiple_of(at * ROWS, ROWS), ROWS) for at in (flip, 1 - flip)]
    firsts = [
        pltpu.make_async_copy(part_ref.at[s], out_hbm.at[rows[s], 0 : FIRST_HEADS * width], part_sem.at[s])
        for s in range(2)
    ]
    for copy in firsts:
        copy.start()
    backs = [jnp.max(reach[s]) for s in range(2)]

    tiles, wide = SHARE // TILE_HEADS, TILE_HEADS * HEAD_DIM

    def put(s, tile):
        cols = slice(tile * wide, (tile + 1) * wide)
        to = pl.ds(FIRST_HEADS * width + tile * wide, wide)
        return pltpu.make_async_copy(o_ref.at[s, :, cols], out_hbm.at[rows[s], to], out_sem.at[s, tile])

    for s in (1, 0):

        def write(a, mixed, s=s):
            o_ref[s, :, a * HEAD_DIM : (a + 1) * HEAD_DIM] = mixed
            if a % TILE_HEADS == TILE_HEADS - 1:
                put(s, a // TILE_HEADS).start()

        def take(base, s=s, write=write):
            attend(
                q_ref, query_side.at[s], key_side.at[s], win.at[s, FIRST_HEADS], FIRST_HEADS, s * ROWS, write, base
            )

        back = backs[s]
        pl.when(back >= 320)(lambda take=take: take(320))
        pl.when(jnp.logical_and(back >= 64, back < 320))(lambda take=take: take(64))
        pl.when(back < 64)(lambda take=take: take(0))
    for copy in firsts:
        copy.wait()
    for s in range(2):
        for tile in range(tiles):
            put(s, tile).wait()


def attention(block_order, doc_lengths, queries, keys, values):
    held = pl.BlockSpec(memory_space=pltpu.HBM)
    near = pl.BlockSpec(memory_space=pltpu.VMEM)
    width = SHARE * HEAD_DIM
    flops = 2 * ROWS * SHARE * KEYS * 512
    operands = [
        pltpu.with_memory_space_constraint(a, pltpu.HBM) for a in (block_order, doc_lengths, queries, keys, values)
    ]
    parts = pl.pallas_call(
        kernel,
        out_shape=(
            pltpu.VMEM((2, ROWS, FIRST_HEADS * width), jnp.float32),
            pltpu.VMEM((2, KV_HEADS, OWN + 1, 2, ROWS, 2 * HEAD_DIM), jnp.bfloat16),
            pltpu.VMEM(queries.shape, jnp.bfloat16),
            pltpu.VMEM((2, KEYS, HEAD_DIM), jnp.bfloat16),
            pltpu.VMEM((2, ROWS, HEAD_DIM), jnp.bfloat16),
            pltpu.VMEM((3, 8, 128), jnp.float32),
        ),
        in_specs=[held] * 5,
        out_specs=(near,) * 6,
        scratch_shapes=[
            pltpu.SMEM((2, 64), jnp.int32),
            pltpu.SMEM((NDOCS,), jnp.int32),
            pltpu.VMEM((2 * ROWS, KV_HEADS * HEAD_DIM), jnp.bfloat16),
            pltpu.VMEM((2 * ROWS, KV_HEADS * HEAD_DIM), jnp.bfloat16),
            pltpu.SemaphoreType.DMA((5,)),
            pltpu.SemaphoreType.DMA((2, KV_HEADS, 9)),
            pltpu.SemaphoreType.DMA((2, KV_HEADS, 8)),
            pltpu.SemaphoreType.DMA((2, 2, KV_HEADS)),
        ],
        compiler_params=pltpu.CompilerParams(collective_id=0, has_side_effects=True, vmem_limit_bytes=32 << 20),
        cost_estimate=pl.CostEstimate(flops=2 * FIRST_HEADS * flops, bytes_accessed=4 << 20, transcendentals=0),
        name="exchange_attend",
    )(*operands)
    return pl.pallas_call(
        last_kernel,
        out_shape=jax.ShapeDtypeStruct(queries.shape, jnp.float32),
        in_specs=[near] * 6,
        out_specs=held,
        scratch_shapes=[
            pltpu.VMEM((2, ROWS, width), jnp.float32),
            pltpu.SemaphoreType.DMA((2,)),
            pltpu.SemaphoreType.DMA((2, SHARE // TILE_HEADS)),
        ],
        compiler_params=pltpu.CompilerParams(vmem_limit_bytes=32 << 20),
        cost_estimate=pl.CostEstimate(flops=2 * (KV_HEADS - FIRST_HEADS) * flops, bytes_accessed=4 << 20, transcendentals=0),
        name="attend_last",
    )(*parts)


def body(queries, keys, values, block_order, doc_lengths):
    return attention(block_order.T, doc_lengths, queries, keys, values)


def solution(mesh):
    rows = P(("wide", "narrow"), None)
    return jax.shard_map(
        body, mesh=mesh, in_specs=(rows, rows, rows, P(), P()), out_specs=rows, check_vma=False
    )
```

time: 36.3 us -> 35.7 us (0.983)
  Pallas kernels: 36.2 us -> 35.5 us
    pallas_call x1, Pallas kernels: 4.36 us -> 2.91 us  [attention(): pl.pallas_call(last_kernel, out_shape=jax.ShapeDtypeStruct(queries.shape,...]
    pallas_call x1, Pallas kernels: 31.9 us -> 32.6 us  [attention(): pl.pallas_call(kernel, out_shape=(pltpu.VMEM((2, ROWS, FIRST_HEADS * widt...]
where the time goes in v3:
time: 35.7 us; the launch traced here: 35.5 us
  Pallas kernels  35.5 us (99%)
    pallas_call x1, Pallas kernels, attention(): pl.pallas_call(kernel, out_shape=(pltpu.VMEM((2, ROWS, FIRST_HEADS * widt...  32.6 us
    pallas_call x1, Pallas kernels, attention(): pl.pallas_call(last_kernel, out_shape=jax.ShapeDtypeStruct(queries.shape,...  2.91 us

profile of v3, /device:TPU:6, one launch (start us, length us, event | category | flops | bytes accessed | tf_op | source)
XLA Modules:
  0.0 35.5 jit_solution(364510621051461913)
XLA Ops:
  0.0 32.6 %exchange_attend.1 = (f32[2,64,6144]{2,1,0:T(8,128)S(1)}, bf16[2,4,7,2,64,256]{5,4,3,2,1,0:T(8,128)(2,1)S(1)}, bf16[128,8192]{1,0:T(8,128)(2,1)S(1)}, bf16[2,832...) custom-call(s32[2,64]{1,0:T(2,128)} %bitcast.1, s32[64]{0:T(128)} %lengths_hbm.1, ...), custom_call_target="tpu_custom_call" | custom-call | flops 5234491392 | bytes 4194304 | tf_op jit(solution)/shard_map/exchange_attend/pallas_call | solution.py:465
  32.6 2.9 %attend_last.1 = f32[128,8192]{1,0:T(8,128)} custom-call(f32[2,64,6144]{2,1,0:T(8,128)S(1)} %get-tuple-element.11.part_ref, bf16[2,4,7,2,64,256]{5,4,3,2,1,0:T(8,128)(2,1)S(1)} %get-tuple-element.12.win, bf16[128,8192]{1,0:T(8,128)(2,1)S(1)} %get-tuple-element.13.q_ref, bf16[2,832,128]{2,1,0:T(8,128)(2,1)S(1)} %get-tuple-element.14.key_side, ...), custom_call_target="tpu_custom_call" | custom-call | flops 1744830464 | bytes 4194304 | tf_op jit(solution)/shard_map/attend_last/pallas_call | solution.py:491

commit v4 on v2

--- a/solution.py
+++ b/solution.py
@@ -18,6 +18,7 @@
 CHUNKS = 13
 KEYS = CHUNKS * ROWS
 NDOCS = 64
+FIRST_HEADS = KV_HEADS - 1
 OWN = 6
 FLOW = 7
 LAST = 31
@@ -229,7 +230,7 @@
     pl.semaphore_wait(barrier, 3 + up + down + turn)
 
 
-def masks(start, lengths_ref, key_side, query_side):
+def masks(start, lengths_ref, key_side, query_side, reach):
     lane = lax.broadcasted_iota(jnp.int32, (1, 128), 1)
     begins = jnp.zeros((1, 128), jnp.int32)
     ends = jnp.zeros((1, 128), jnp.int32)
@@ -237,6 +238,8 @@
         length = lengths_ref[e]
         begins = begins + jnp.where(lane > e, length, 0)
         ends = ends + jnp.where(lane >= e, length, 0)
+    back = jnp.where(begins <= start, begins, 0) - (start - (KEYS - ROWS))
+    reach[...] = jnp.broadcast_to(back, (8, 128)).astype(jnp.float32)
     lanes = lax.broadcasted_iota(jnp.int32, (KEYS, 128), 1)
     place = lax.broadcasted_iota(jnp.int32, (KEYS, 128), 0) - (KEYS - ROWS)
     pos = place + start
@@ -255,14 +258,19 @@
 PARTS = ((0, 256), (256, 512), (512, 768), (768, 896))
 
 
-def attend(q_ref, side_ref, keys_side_ref, win_ref, h, row, write):
+def attend(q_ref, side_ref, keys_side_ref, win_ref, h, row, write, base=0):
     rate = math.log2(math.e) / math.sqrt(HEAD_DIM)
     k = win_ref[:, :, 0:HEAD_DIM].reshape(KEYS, HEAD_DIM)
     v = win_ref[:, :, HEAD_DIM : 2 * HEAD_DIM].reshape(KEYS, HEAD_DIM)
     k = jnp.concatenate([k, keys_side_ref[...]], axis=1)
     v = jnp.concatenate([v, jnp.ones((KEYS, HEAD_DIM), jnp.bfloat16)], axis=1)
-    k = jnp.concatenate([k, k[KEYS - ROWS :]], axis=0)
-    v = jnp.concatenate([v, jnp.zeros((ROWS, 2 * HEAD_DIM), jnp.bfloat16)], axis=0)
+    if base:
+        k, v = k[base:], v[base:]
+        parts = [(at, at + 256) for at in range(0, KEYS - base, 256)]
+    else:
+        k = jnp.concatenate([k, k[KEYS - ROWS :]], axis=0)
+        v = jnp.concatenate([v, jnp.zeros((ROWS, 2 * HEAD_DIM), jnp.bfloat16)], axis=0)
+        parts = PARTS
     side = side_ref[...]
     tiles = SHARE // TILE_HEADS
 
@@ -280,7 +288,7 @@
         return lax.dot_general(q, k[low:high], (((1,), (1,)), ((), ())), preferred_element_type=jnp.float32)
 
     q = queries(0)
-    ahead = [score(q, part) for part in PARTS]
+    ahead = [score(q, part) for part in parts]
     for t in range(tiles):
         scores, ahead = ahead, []
         if t + 1 < tiles:
@@ -290,7 +298,7 @@
         )
         top = jnp.max(top, axis=1, keepdims=True)
         mixed = None
-        for part, s in zip(PARTS, scores):
+        for part, s in zip(parts, scores):
             if t + 1 < tiles:
                 ahead.append(score(q, part))
             weights = jnp.exp2((s - top) * rate).astype(jnp.bfloat16)
@@ -302,8 +310,8 @@
 
 
 def kernel(
-    order_hbm, lengths_hbm, q_hbm, k_hbm, v_hbm, out_ref, win, q_ref, key_side, query_side, order_ref, lengths_ref, k_ref,
-    v_ref, in_sem, send_sem, recv_sem, sib_sem,
+    order_hbm, lengths_hbm, q_hbm, k_hbm, v_hbm, out_ref, win, q_ref, key_side, query_side, reach, order_ref, lengths_ref,
+    k_ref, v_ref, in_sem, send_sem, recv_sem, sib_sem,
 ):
     p = Place()
     loads = [
@@ -318,6 +326,7 @@
     for load in loads[:4]:
         load.wait()
     first = order_ref[0, p.w]
+    reach[2] = jnp.full((8, 128), first, jnp.int32).astype(jnp.float32)
 
     def swapped(width):
         return jnp.full((ROWS, width), first, jnp.int32) >= 64
@@ -361,8 +370,8 @@
 
         @pl.when(t == 0)
         def _():
-            masks(p.w * GROUP + p.n * ROWS, lengths_ref, key_side.at[0], query_side.at[0])
-            masks((2 * 64 - 1 - p.w) * GROUP + p.n * ROWS, lengths_ref, key_side.at[1], query_side.at[1])
+            masks(p.w * GROUP + p.n * ROWS, lengths_ref, key_side.at[0], query_side.at[0], reach.at[0])
+            masks((2 * 64 - 1 - p.w) * GROUP + p.n * ROWS, lengths_ref, key_side.at[1], query_side.at[1], reach.at[1])
 
         @pl.when(t == 1)
         def _():
@@ -395,34 +404,46 @@
     lax.fori_loop(0, KV_HEADS, drain, 0)
 
 
-def last_kernel(order_hbm, part_ref, win, q_ref, key_side, query_side, out_hbm, order_ref, o_ref, in_sem, out_sem):
-    load = pltpu.make_async_copy(order_hbm, order_ref, in_sem)
-    load.start()
+def last_kernel(part_ref, win, q_ref, key_side, query_side, reach, out_hbm, o_ref, part_sem, out_sem):
     width = SHARE * HEAD_DIM
-    done = (KV_HEADS - 1) * width
-    w = lax.axis_index("wide")
-
-    def unit(s):
-        def write(a, mixed):
+    flip = (jnp.max(reach[2]) >= 64).astype(jnp.int32)
+    rows = [pl.ds(pl.multiple_of(at * ROWS, ROWS), ROWS) for at in (flip, 1 - flip)]
+    firsts = [
+        pltpu.make_async_copy(part_ref.at[s], out_hbm.at[rows[s], 0 : FIRST_HEADS * width], part_sem.at[s])
+        for s in range(2)
+    ]
+    for copy in firsts:
+        copy.start()
+    backs = [jnp.max(reach[s]) for s in range(2)]
+
+    tiles, wide = SHARE // TILE_HEADS, TILE_HEADS * HEAD_DIM
+
+    def put(s, tile):
+        cols = slice(tile * wide, (tile + 1) * wide)
+        to = pl.ds(FIRST_HEADS * width + tile * wide, wide)
+        return pltpu.make_async_copy(o_ref.at[s, :, cols], out_hbm.at[rows[s], to], out_sem.at[s, tile])
+
+    for s in (1, 0):
+
+        def write(a, mixed, s=s):
             o_ref[s, :, a * HEAD_DIM : (a + 1) * HEAD_DIM] = mixed
-
-        attend(
-            q_ref, query_side.at[s], key_side.at[s], win.at[s, KV_HEADS - 1, 0:CHUNKS], KV_HEADS - 1, s * ROWS, write
-        )
-
-    unit(1)
-    load.wait()
-    flip = (order_ref[0, w] >= 64).astype(jnp.int32)
-    rows = [pl.ds(pl.multiple_of(at * ROWS, ROWS), ROWS) for at in (flip, 1 - flip)]
-    copies = [
-        pltpu.make_async_copy(part_ref.at[s], out_hbm.at[rows[s], 0:done], out_sem.at[s]) for s in range(2)
-    ] + [pltpu.make_async_copy(o_ref.at[s], out_hbm.at[rows[s], done : done + width], out_sem.at[2 + s]) for s in range(2)]
-    for i in (3, 1, 0):
-        copies[i].start()
-    unit(0)
-    copies[2].start()
-    for copy in copies:
+            if a % TILE_HEADS == TILE_HEADS - 1:
+                put(s, a // TILE_HEADS).start()
+
+        def take(base, s=s, write=write):
+            attend(
+                q_ref, query_side.at[s], key_side.at[s], win.at[s, FIRST_HEADS, 0:CHUNKS], FIRST_HEADS, s * ROWS, write, base
+            )
+
+        back = backs[s]
+        pl.when(back >= 320)(lambda take=take: take(320))
+        pl.when(jnp.logical_and(back >= 64, back < 320))(lambda take=take: take(64))
+        pl.when(back < 64)(lambda take=take: take(0))
+    for copy in firsts:
         copy.wait()
+    for s in range(2):
+        for tile in range(tiles):
+            put(s, tile).wait()
 
 
 def attention(block_order, doc_lengths, queries, keys, values):
@@ -436,14 +457,15 @@
     parts = pl.pallas_call(
         kernel,
         out_shape=(
-            pltpu.VMEM((2, ROWS, (KV_HEADS - 1) * width), jnp.float32),
+            pltpu.VMEM((2, ROWS, FIRST_HEADS * width), jnp.float32),
             pltpu.VMEM((2, KV_HEADS, CHUNKS + 1, ROWS, 2 * HEAD_DIM), jnp.bfloat16),
             pltpu.VMEM(queries.shape, jnp.bfloat16),
             pltpu.VMEM((2, KEYS, HEAD_DIM), jnp.bfloat16),
             pltpu.VMEM((2, ROWS, HEAD_DIM), jnp.bfloat16),
+            pltpu.VMEM((3, 8, 128), jnp.float32),
         ),
         in_specs=[held] * 5,
-        out_specs=(near,) * 5,
+        out_specs=(near,) * 6,
         scratch_shapes=[
             pltpu.SMEM((2, 64), jnp.int32),
             pltpu.SMEM((NDOCS,), jnp.int32),
@@ -455,24 +477,23 @@
             pltpu.SemaphoreType.DMA((2, 2, KV_HEADS)),
         ],
         compiler_params=pltpu.CompilerParams(collective_id=0, has_side_effects=True, vmem_limit_bytes=32 << 20),
-        cost_estimate=pl.CostEstimate(flops=6 * flops, bytes_accessed=4 << 20, transcendentals=0),
+        cost_estimate=pl.CostEstimate(flops=2 * FIRST_HEADS * flops, bytes_accessed=4 << 20, transcendentals=0),
         name="exchange_attend",
     )(*operands)
     return pl.pallas_call(
         last_kernel,
         out_shape=jax.ShapeDtypeStruct(queries.shape, jnp.float32),
-        in_specs=[held] + [near] * 5,
+        in_specs=[near] * 6,
         out_specs=held,
         scratch_shapes=[
-            pltpu.SMEM((2, 64), jnp.int32),
             pltpu.VMEM((2, ROWS, width), jnp.float32),
-            pltpu.SemaphoreType.DMA,
-            pltpu.SemaphoreType.DMA((4,)),
+            pltpu.SemaphoreType.DMA((2,)),
+            pltpu.SemaphoreType.DMA((2, SHARE // TILE_HEADS)),
         ],
         compiler_params=pltpu.CompilerParams(vmem_limit_bytes=32 << 20),
-        cost_estimate=pl.CostEstimate(flops=2 * flops, bytes_accessed=4 << 20, transcendentals=0),
+        cost_estimate=pl.CostEstimate(flops=2 * (KV_HEADS - FIRST_HEADS) * flops, bytes_accessed=4 << 20, transcendentals=0),
         name="attend_last",
-    )(operands[0], *parts)
+    )(*parts)
 
 
 def body(queries, keys, values, block_order, doc_lengths):

time: 36.3 us -> 35.5 us (0.978)
  Pallas kernels: 36.2 us -> 35.1 us
    pallas_call x1, Pallas kernels: 4.36 us -> 3.28 us  [attention(): pl.pallas_call(last_kernel, out_shape=jax.ShapeDtypeStruct(queries.shape,...]
where the time goes in v4:
time: 35.5 us; the launch traced here: 35.1 us
  Pallas kernels  35.1 us (99%)
    pallas_call x1, Pallas kernels, attention(): pl.pallas_call(kernel, out_shape=(pltpu.VMEM((2, ROWS, FIRST_HEADS * widt...  31.9 us
    pallas_call x1, Pallas kernels, attention(): pl.pallas_call(last_kernel, out_shape=jax.ShapeDtypeStruct(queries.shape,...  3.28 us

profile of v4, /device:TPU:6, one launch (start us, length us, event | category | flops | bytes accessed | tf_op | source)
XLA Modules:
  0.0 35.1 jit_solution(15442382779561119223)
XLA Ops:
  0.0 31.9 %exchange_attend.1 = (f32[2,64,6144]{2,1,0:T(8,128)S(1)}, bf16[2,4,14,64,256]{4,3,2,1,0:T(8,128)(2,1)S(1)}, bf16[128,8192]{1,0:T(8,128)(2,1)S(1)}, bf16[2,832,12...) custom-call(s32[2,64]{1,0:T(2,128)} %bitcast.1, s32[64]{0:T(128)} %lengths_hbm.1, ...), custom_call_target="tpu_custom_call" | custom-call | flops 5234491392 | bytes 4194304 | tf_op jit(solution)/shard_map/exchange_attend/pallas_call | solution.py:457
  31.9 3.3 %attend_last.1 = f32[128,8192]{1,0:T(8,128)} custom-call(f32[2,64,6144]{2,1,0:T(8,128)S(1)} %get-tuple-element.11.part_ref, bf16[2,4,14,64,256]{4,3,2,1,0:T(8,128)(2,1)S(1)} %get-tuple-element.12.win, bf16[128,8192]{1,0:T(8,128)(2,1)S(1)} %get-tuple-element.13.q_ref, bf16[2,832,128]{2,1,0:T(8,128)(2,1)S(1)} %get-tuple-element.14.key_side, ...), custom_call_target="tpu_custom_call" | custom-call | flops 1744830464 | bytes 4194304 | tf_op jit(solution)/shard_map/attend_last/pallas_call | solution.py:483

commit v5 on v4

--- a/solution.py
+++ b/solution.py
@@ -362,7 +362,7 @@
         attend(q_ref, query_side.at[s], key_side.at[s], win.at[s, h, 0:CHUNKS], h, s * ROWS, write)
 
     def both(number, h):
-        for s in range(2):
+        for s in (1, 0):
             ex.phase(number, s, h)
 
     def fill(t, carry):

time: 35.5 us -> 35.7 us (level)
  Pallas kernels: 35.1 us -> 35.5 us
    pallas_call x1, Pallas kernels: 31.9 us -> 32.5 us  [attention(): pl.pallas_call(kernel, out_shape=(pltpu.VMEM((2, ROWS, FIRST_HEADS * widt...]
    pallas_call x1, Pallas kernels: 3.28 us -> 2.91 us  [attention(): pl.pallas_call(last_kernel, out_shape=jax.ShapeDtypeStruct(queries.shape,...]
where the time goes in v5:
time: 35.7 us; the launch traced here: 35.5 us
  Pallas kernels  35.5 us (99%)
    pallas_call x1, Pallas kernels, attention(): pl.pallas_call(kernel, out_shape=(pltpu.VMEM((2, ROWS, FIRST_HEADS * widt...  32.5 us
    pallas_call x1, Pallas kernels, attention(): pl.pallas_call(last_kernel, out_shape=jax.ShapeDtypeStruct(queries.shape,...  2.91 us

profile of v5, /device:TPU:6, one launch (start us, length us, event | category | flops | bytes accessed | tf_op | source)
XLA Modules:
  0.0 35.5 jit_solution(12375481212507915125)
XLA Ops:
  0.0 32.5 %exchange_attend.1 = (f32[2,64,6144]{2,1,0:T(8,128)S(1)}, bf16[2,4,14,64,256]{4,3,2,1,0:T(8,128)(2,1)S(1)}, bf16[128,8192]{1,0:T(8,128)(2,1)S(1)}, bf16[2,832,12...) custom-call(s32[2,64]{1,0:T(2,128)} %bitcast.1, s32[64]{0:T(128)} %lengths_hbm.1, ...), custom_call_target="tpu_custom_call" | custom-call | flops 5234491392 | bytes 4194304 | tf_op jit(solution)/shard_map/exchange_attend/pallas_call | solution.py:457
  32.6 2.9 %attend_last.1 = f32[128,8192]{1,0:T(8,128)} custom-call(f32[2,64,6144]{2,1,0:T(8,128)S(1)} %get-tuple-element.11.part_ref, bf16[2,4,14,64,256]{4,3,2,1,0:T(8,128)(2,1)S(1)} %get-tuple-element.12.win, bf16[128,8192]{1,0:T(8,128)(2,1)S(1)} %get-tuple-element.13.q_ref, bf16[2,832,128]{2,1,0:T(8,128)(2,1)S(1)} %get-tuple-element.14.key_side, ...), custom_call_target="tpu_custom_call" | custom-call | flops 1744830464 | bytes 4194304 | tf_op jit(solution)/shard_map/attend_last/pallas_call | solution.py:483
